TPU v7x, 512 devices: a whole 4x4x16 slice. The times are simulated.
512 devices in a mesh: dp: 128 (over x, z, y_hi), mp: 4 (over y_lo, core).
Axes of the slice: x: 4, y: 4 (y_hi: 2, y_lo: 2; y = y_hi * 2 + y_lo), z: 16, core: 2. Of those that a mesh axis runs over, the one named last changes fastest.
Arguments:
- picture_encoder_outputs: bfloat16 [24576, 1536], P('dp', 'mp'), may hold values from -100 to 100
- caption_encoder_outputs: bfloat16 [24576, 1536], P('dp', 'mp'), may hold values from -100 to 100
- picture_mapping_matrix: bfloat16 [1536, 1536], P('mp'), may hold values from -0.15625 to 0.15625
- caption_mapping_matrix: bfloat16 [1536, 1536], P('mp'), may hold values from -0.15625 to 0.15625
- scale_exponent_param: float32 [1], replicated, may hold values from 3 to 4
- score_shift_param: float32 [1], replicated, may hold values from -3 to -1
- partner_caption_row: int32 [128, 192], P('dp'), may hold values from 0 to 191, each once within a row
Outputs:
- img_grad: bfloat16 [24576, 1536], P('dp', 'mp')
- txt_grad: bfloat16 [24576, 1536], P('dp', 'mp')
- row_loss: float32 [24576], P('dp')
Inputs may be any that keep to these rules, and one draw needn't show every extreme that they name: `partner_caption_row`: each row of 192 entries names every row of its block once.
All inputs are finite; a program needn't handle non-finite values.
Results may differ from a plain program's by a relative error of at most 0.018.
Values may be sent and summed in bfloat16 or wider, within the bound.
A program may use at most 64 MiB of HBM per device.

v0:
```python
import jax
import jax.numpy as jnp
from jax import lax
from jax.sharding import PartitionSpec as P

STEPS = 8


norm_eps = 1e-06


def from_behind(value, axis, by):
    peers = lax.axis_size(axis)
    return lax.ppermute(value, axis, [(i, (i + by) % peers) for i in range(peers)])


def shards(
    picture_encoder_outputs,
    caption_encoder_outputs,
    picture_mapping_matrix,
    caption_mapping_matrix,
    scale_exponent_param,
    score_shift_param,
    partner_caption_row,
):
    mp_count = lax.axis_size("mp")
    share_rows = picture_mapping_matrix.shape[1] // mp_count
    pair_rows = picture_encoder_outputs.shape[0]
    img_slice = picture_mapping_matrix
    txt_slice = caption_mapping_matrix
    img_term = lax.dot_general(
        img_slice,
        picture_encoder_outputs,
        (((0,), (1,)), ((), ())),
        preferred_element_type=jnp.float32,
    )
    txt_term = lax.dot_general(
        txt_slice,
        caption_encoder_outputs,
        (((0,), (1,)), ((), ())),
        preferred_element_type=jnp.float32,
    )
    embeddings = lax.psum_scatter(
        jnp.stack([img_term, txt_term], axis=1), "mp", scatter_dimension=0, tiled=True
    )
    squares = lax.psum(jnp.sum(embeddings * embeddings, axis=0), "mp")
    radius = jnp.sqrt(squares + norm_eps)
    unit_vecs = embeddings / radius[None]
    img_emb = unit_vecs[:, 0].astype(jnp.bfloat16)
    txt_emb = unit_vecs[:, 1].astype(jnp.bfloat16)
    partners = [txt_emb]
    for offset in range(1, STEPS):
        partners.append(from_behind(partners[-1], "dp", -1))

    def partial_tile(partner):
        return lax.dot_general(
            img_emb, partner, (((0,), (0,)), ((), ())), preferred_element_type=jnp.float32
        )

    score_scale_factor = jnp.exp(scale_exponent_param[0])
    score_shift_scalar = score_shift_param[0]
    positive = partner_caption_row[0][:, None] == lax.iota(jnp.int32, pair_rows)[None, :]
    slopes = []
    cosines = [
        lax.psum(partial_tile(partner).astype(jnp.bfloat16), "mp").astype(jnp.float32)
        for partner in partners
    ]
    row_total = jnp.zeros((pair_rows,), jnp.float32)
    for offset in range(STEPS):
        angular_agreement = cosines[offset]
        matched_scores = score_scale_factor * angular_agreement + score_shift_scalar
        if offset == 0:
            match_polarity = jnp.where(positive, 1.0, -1.0).astype(jnp.float32)
        else:
            match_polarity = -jnp.ones_like(matched_scores)
        loss_part = jnp.sum(jax.nn.softplus(-match_polarity * matched_scores), axis=1)
        squash_derivative = (
            -score_scale_factor * match_polarity * jax.nn.sigmoid(-match_polarity * matched_scores)
        ).astype(jnp.bfloat16)
        loss_part, squash_derivative = (loss_part, squash_derivative)
        row_total = row_total + loss_part
        slopes.append(squash_derivative)
    img_step = jnp.zeros((share_rows, pair_rows), jnp.float32)
    text_terms = []
    for offset in range(STEPS):
        squash_derivative = slopes[offset]
        img_step = img_step + lax.dot_general(
            partners[offset],
            squash_derivative,
            (((1,), (1,)), ((), ())),
            preferred_element_type=jnp.float32,
        )
        text_terms.append(jnp.dot(img_emb, squash_derivative, preferred_element_type=jnp.float32))
    carried = text_terms[STEPS - 1]
    for offset in range(STEPS - 2, -1, -1):
        carried = from_behind(carried, "dp", 1) + text_terms[offset]
    row_loss = row_total / (STEPS * pair_rows)
    step_pair = jnp.stack([img_step, carried], axis=1)
    radial_dots = lax.psum(jnp.sum(unit_vecs * step_pair, axis=0), "mp")
    delta_rows = ((step_pair - unit_vecs * radial_dots[None]) / radius[None]).astype(jnp.bfloat16)
    gathered = lax.all_gather(delta_rows, "mp", axis=0, tiled=True)
    img_slice = picture_mapping_matrix
    txt_slice = caption_mapping_matrix
    img_more = lax.dot_general(
        gathered[:, 0], img_slice, (((0,), (1,)), ((), ())), preferred_element_type=jnp.float32
    )
    txt_more = lax.dot_general(
        gathered[:, 1], txt_slice, (((0,), (1,)), ((), ())), preferred_element_type=jnp.float32
    )
    return (img_more.astype(jnp.bfloat16), txt_more.astype(jnp.bfloat16), row_loss)


def solution(mesh):
    placed = (P("dp", "mp"), P("dp", "mp"), P("mp", None), P("mp", None), P(), P(), P("dp", None))
    return jax.shard_map(
        shards,
        mesh=mesh,
        in_specs=placed,
        out_specs=(P("dp", "mp"), P("dp", "mp"), P("dp")),
        check_vma=False,
    )
```

profile of v0, /device:TPU:1, one launch (start us, length us, event | category | flops | bytes accessed | tf_op | source)
XLA Modules:
  0.0 348.1 jit_solution(10886112263101333164)
XLA Ops:
  8.4 1.4 convolution_bitcast_fusion
  10.3 1.6 pad_maximum_fusion
  11.9 43.7 %reduce-scatter.2.cloned.1.call-done = f32[384,2,192]{0,2,1:T(8,128)} async-done(((f32[1536,2,192]{0,2,1:T(8,128)}), f32[384,2,192]{0,2,1:T(8,128)}) %reduce-scatter.2.cloned.1.call-update) | async-done | bytes 589840 | tf_op jit(solution)/shard_map/reduce_scatter | solution.py:43
  56.9 5.4 %psum.70 = f32[2,192]{1,0:T(2,128)S(1)} all-reduce(f32[2,192]{1,0:T(2,128)S(1)} %multiply_reduce_fusion.1), channel_id=1, replica_groups=mesh['dp'=128,'mp'=4] {'mp'}, use_global_device_ids=true, to_apply=%region_2.0 | all-reduce | flops 384 | bytes 3072 | tf_op jit(solution)/shard_map/psum | solution.py:46
  63.6 9.9 %collective-permute-start = (bf16[384,192]{0,1:T(8,128)(2,1)S(1)}, bf16[384,192]{0,1:T(8,128)(2,1)S(1)}, u32[]{:S(2)}, u32[]{:S(2)}) collective-permute-start(bf16[384,192]{0,1:T(8,128)(2,1)S(1)} %get-tuple-element.11), channel_id=1, source_target_pairs={{0,508},{4,0},{8,4},{12,8},{16,12},{20,16},{24,20},{28,24},{32,28}... | collective-permute-start | bytes 442376 | tf_op jit(solution)/shard_map/ppermute | solution.py:14
  75.6 9.5 %collective-permute-start.1 = (bf16[384,192]{0,1:T(8,128)(2,1)S(1)}, bf16[384,192]{0,1:T(8,128)(2,1)S(1)}, u32[]{:S(2)}, u32[]{:S(2)}) collective-permute-start(bf16[384,192]{0,1:T(8,128)(2,1)S(1)} %collective-permute-done), channel_id=1, source_target_pairs={{0,508},{4,0},{8,4},{12,8},{16,12},{20,16},{24,20},{28,24},{32,28}... | collective-permute-start | bytes 442376 | tf_op jit(solution)/shard_map/ppermute | solution.py:14
  87.2 9.5 %collective-permute-start.2 = (bf16[384,192]{0,1:T(8,128)(2,1)S(1)}, bf16[384,192]{0,1:T(8,128)(2,1)S(1)}, u32[]{:S(2)}, u32[]{:S(2)}) collective-permute-start(bf16[384,192]{0,1:T(8,128)(2,1)S(1)} %collective-permute-done.1), channel_id=1, source_target_pairs={{0,508},{4,0},{8,4},{12,8},{16,12},{20,16},{24,20},{28,24},{32,28}... | collective-permute-start | bytes 442376 | tf_op jit(solution)/shard_map/ppermute | solution.py:14
  98.8 9.5 %collective-permute-start.3 = (bf16[384,192]{0,1:T(8,128)(2,1)S(1)}, bf16[384,192]{0,1:T(8,128)(2,1)S(1)}, u32[]{:S(2)}, u32[]{:S(2)}) collective-permute-start(bf16[384,192]{0,1:T(8,128)(2,1)S(1)} %collective-permute-done.2), channel_id=1, source_target_pairs={{0,508},{4,0},{8,4},{12,8},{16,12},{20,16},{24,20},{28,24},{32,28}... | collective-permute-start | bytes 442376 | tf_op jit(solution)/shard_map/ppermute | solution.py:14
  110.4 9.5 %collective-permute-start.4 = (bf16[384,192]{0,1:T(8,128)(2,1)S(1)}, bf16[384,192]{0,1:T(8,128)(2,1)S(1)}, u32[]{:S(2)}, u32[]{:S(2)}) collective-permute-start(bf16[384,192]{0,1:T(8,128)(2,1)S(1)} %collective-permute-done.3), channel_id=1, source_target_pairs={{0,508},{4,0},{8,4},{12,8},{16,12},{20,16},{24,20},{28,24},{32,28}... | collective-permute-start | bytes 442376 | tf_op jit(solution)/shard_map/ppermute | solution.py:14
  122.0 9.5 %collective-permute-start.5 = (bf16[384,192]{0,1:T(8,128)(2,1)S(1)}, bf16[384,192]{0,1:T(8,128)(2,1)S(1)}, u32[]{:S(2)}, u32[]{:S(2)}) collective-permute-start(bf16[384,192]{0,1:T(8,128)(2,1)S(1)} %collective-permute-done.4), channel_id=1, source_target_pairs={{0,508},{4,0},{8,4},{12,8},{16,12},{20,16},{24,20},{28,24},{32,28}... | collective-permute-start | bytes 442376 | tf_op jit(solution)/shard_map/ppermute | solution.py:14
  133.6 9.5 %collective-permute-start.6 = (bf16[384,192]{0,1:T(8,128)(2,1)S(1)}, bf16[384,192]{0,1:T(8,128)(2,1)S(1)}, u32[]{:S(2)}, u32[]{:S(2)}) collective-permute-start(bf16[384,192]{0,1:T(8,128)(2,1)S(1)} %collective-permute-done.5), channel_id=1, source_target_pairs={{0,508},{4,0},{8,4},{12,8},{16,12},{20,16},{24,20},{28,24},{32,28}... | collective-permute-start | bytes 442376 | tf_op jit(solution)/shard_map/ppermute | solution.py:14
  147.5 56.8 %all-reduce.3.cloned.1.call-done = (bf16[192,192]{1,0:T(8,128)(2,1)}, bf16[192,192]{1,0:T(8,128)(2,1)}, bf16[192,192]{1,0:T(8,128)(2,1)}, bf16[192,192]{1,0:T(8,...) async-done(((bf16[192,192]{1,0:T(8,128)(2,1)}, bf16[192,192]{1,0:T(8,128)(2,1)}, ...) | async-done | bytes 589840 | tf_op jit(solution)/shard_map/psum | solution.py:65
  205.5 4.2 %collective-permute-start.7 = (f32[384,192]{0,1:T(8,128)S(1)}, f32[384,192]{0,1:T(8,128)S(1)}, u32[]{:S(2)}, u32[]{:S(2)}) collective-permute-start(f32[384,192]{0,1:T(8,128)S(1)} %fusion.19), channel_id=1, source_target_pairs={{0,4},{4,8},{8,12},{12,16},{16,20},{20,24},{24,28},{28,32},{32,36}... | collective-permute-start | bytes 884744 | tf_op jit(solution)/shard_map/ppermute | solution.py:14
  211.3 11.4 %collective-permute-done.7 = f32[384,192]{0,1:T(8,128)S(1)} collective-permute-done((f32[384,192]{0,1:T(8,128)S(1)}, f32[384,192]{0,1:T(8,128)S(1)}, u32[]{:S(2)}, u32[]{:S(2)}) %collective-permute-start.7) | collective-permute-done | bytes 294944 | tf_op jit(solution)/shard_map/ppermute | solution.py:14
  222.9 1.9 collective-permute-start.8
  225.4 13.0 %collective-permute-done.8 = f32[384,192]{0,1:T(8,128)S(1)} collective-permute-done((f32[384,192]{0,1:T(8,128)S(1)}, f32[384,192]{0,1:T(8,128)S(1)}, u32[]{:S(2)}, u32[]{:S(2)}) %collective-permute-start.8) | collective-permute-done | bytes 294944 | tf_op jit(solution)/shard_map/ppermute | solution.py:14
  238.4 1.9 collective-permute-start.9
  240.9 12.1 %collective-permute-done.9 = f32[384,192]{0,1:T(8,128)S(1)} collective-permute-done((f32[384,192]{0,1:T(8,128)S(1)}, f32[384,192]{0,1:T(8,128)S(1)}, u32[]{:S(2)}, u32[]{:S(2)}) %collective-permute-start.9) | collective-permute-done | bytes 294944 | tf_op jit(solution)/shard_map/ppermute | solution.py:14
  253.0 1.9 collective-permute-start.10
  255.4 11.2 %collective-permute-done.10 = f32[384,192]{0,1:T(8,128)S(1)} collective-permute-done((f32[384,192]{0,1:T(8,128)S(1)}, f32[384,192]{0,1:T(8,128)S(1)}, u32[]{:S(2)}, u32[]{:S(2)}) %collective-permute-start.10) | collective-permute-done | bytes 294944 | tf_op jit(solution)/shard_map/ppermute | solution.py:14
  266.6 1.9 collective-permute-start.11
  269.1 10.8 %collective-permute-done.11 = f32[384,192]{0,1:T(8,128)S(1)} collective-permute-done((f32[384,192]{0,1:T(8,128)S(1)}, f32[384,192]{0,1:T(8,128)S(1)}, u32[]{:S(2)}, u32[]{:S(2)}) %collective-permute-start.11) | collective-permute-done | bytes 294944 | tf_op jit(solution)/shard_map/ppermute | solution.py:14
  279.9 1.9 collective-permute-start.12
  282.3 10.7 %collective-permute-done.12 = f32[384,192]{0,1:T(8,128)S(1)} collective-permute-done((f32[384,192]{0,1:T(8,128)S(1)}, f32[384,192]{0,1:T(8,128)S(1)}, u32[]{:S(2)}, u32[]{:S(2)}) %collective-permute-start.12) | collective-permute-done | bytes 294944 | tf_op jit(solution)/shard_map/ppermute | solution.py:14
  293.1 1.9 collective-permute-start.13
  295.6 10.6 %collective-permute-done.13 = f32[384,192]{0,1:T(8,128)S(1)} collective-permute-done((f32[384,192]{0,1:T(8,128)S(1)}, f32[384,192]{0,1:T(8,128)S(1)}, u32[]{:S(2)}, u32[]{:S(2)}) %collective-permute-start.13) | collective-permute-done | bytes 294944 | tf_op jit(solution)/shard_map/ppermute | solution.py:14
  306.6 12.4 %psum.79 = f32[2,192]{1,0:T(2,128)S(1)} all-reduce(f32[2,192]{1,0:T(2,128)S(1)} %multiply_reduce_fusion), channel_id=1, replica_groups=mesh['dp'=128,'mp'=4] {'mp'}, use_global_device_ids=true, to_apply=%region_12.13 | all-reduce | flops 384 | bytes 3072 | tf_op jit(solution)/shard_map/psum | solution.py:99
  319.0 1.9 divide_convert_fusion
  320.9 1.3 fusion.6
  322.2 1.3 fusion.8
  325.7 12.2 %all-gather.2.cloned.1.call-done = bf16[1536,2,192]{0,2,1:T(8,128)(2,1)} async-done(((bf16[384,2,192]{0,2,1:T(8,128)(2,1)}), bf16[1536,2,192]{0,2,1:T(8,128)(2,1)}) %all-gather.2.cloned.1.call-update) | async-done | bytes 1179664 | tf_op jit(solution)/shard_map/all_gather | solution.py:101
  338.0 2.4 convolution_convert_fusion
  (89 shorter events, 29.7 us)
Async XLA Ops:
  7.2 2.6 copy-start.4
  7.2 2.6 copy-start.2
  7.2 48.5 %reduce-scatter.2.cloned.1.call-start = ((), (), s32[]{:S(2)}) async-start(), calls=%async_computation.1 | async-start | bytes 2949120 | tf_op jit(solution)/shard_map/reduce_scatter | solution.py:43
  11.9 192.4 %all-reduce.3.cloned.1.call-start = ((), (), s32[]{:S(2)}) async-start(), calls=%async_computation.3 | async-start | bytes 1572864 | tf_op jit(solution)/shard_map/psum | solution.py:65
  63.6 12.0 %collective-permute-start = (bf16[384,192]{0,1:T(8,128)(2,1)S(1)}, bf16[384,192]{0,1:T(8,128)(2,1)S(1)}, u32[]{:S(2)}, u32[]{:S(2)}) collective-permute-start(bf16[384,192]{0,1:T(8,128)(2,1)S(1)} %get-tuple-element.11), channel_id=1, source_target_pairs={{0,508},{4,0},{8,4},{12,8},{16,12},{20,16},{24,20},{28,24},{32,28}... | collective-permute-start | bytes 442376 | tf_op jit(solution)/shard_map/ppermute | solution.py:14
  75.6 56.8 %copy-start.5 = (bf16[384,192]{0,1:T(8,128)(2,1)}, bf16[384,192]{0,1:T(8,128)(2,1)S(1)}, u32[]{:S(2)}) copy-start(bf16[384,192]{0,1:T(8,128)(2,1)S(1)} %collective-permute-done) | copy-start | bytes 442372
  75.6 11.6 %collective-permute-start.1 = (bf16[384,192]{0,1:T(8,128)(2,1)S(1)}, bf16[384,192]{0,1:T(8,128)(2,1)S(1)}, u32[]{:S(2)}, u32[]{:S(2)}) collective-permute-start(bf16[384,192]{0,1:T(8,128)(2,1)S(1)} %collective-permute-done), channel_id=1, source_target_pairs={{0,508},{4,0},{8,4},{12,8},{16,12},{20,16},{24,20},{28,24},{32,28}... | collective-permute-start | bytes 442376 | tf_op jit(solution)/shard_map/ppermute | solution.py:14
  87.2 11.6 %collective-permute-start.2 = (bf16[384,192]{0,1:T(8,128)(2,1)S(1)}, bf16[384,192]{0,1:T(8,128)(2,1)S(1)}, u32[]{:S(2)}, u32[]{:S(2)}) collective-permute-start(bf16[384,192]{0,1:T(8,128)(2,1)S(1)} %collective-permute-done.1), channel_id=1, source_target_pairs={{0,508},{4,0},{8,4},{12,8},{16,12},{20,16},{24,20},{28,24},{32,28}... | collective-permute-start | bytes 442376 | tf_op jit(solution)/shard_map/ppermute | solution.py:14
  98.8 11.6 %collective-permute-start.3 = (bf16[384,192]{0,1:T(8,128)(2,1)S(1)}, bf16[384,192]{0,1:T(8,128)(2,1)S(1)}, u32[]{:S(2)}, u32[]{:S(2)}) collective-permute-start(bf16[384,192]{0,1:T(8,128)(2,1)S(1)} %collective-permute-done.2), channel_id=1, source_target_pairs={{0,508},{4,0},{8,4},{12,8},{16,12},{20,16},{24,20},{28,24},{32,28}... | collective-permute-start | bytes 442376 | tf_op jit(solution)/shard_map/ppermute | solution.py:14
  110.4 11.6 %collective-permute-start.4 = (bf16[384,192]{0,1:T(8,128)(2,1)S(1)}, bf16[384,192]{0,1:T(8,128)(2,1)S(1)}, u32[]{:S(2)}, u32[]{:S(2)}) collective-permute-start(bf16[384,192]{0,1:T(8,128)(2,1)S(1)} %collective-permute-done.3), channel_id=1, source_target_pairs={{0,508},{4,0},{8,4},{12,8},{16,12},{20,16},{24,20},{28,24},{32,28}... | collective-permute-start | bytes 442376 | tf_op jit(solution)/shard_map/ppermute | solution.py:14
  122.0 11.6 %collective-permute-start.5 = (bf16[384,192]{0,1:T(8,128)(2,1)S(1)}, bf16[384,192]{0,1:T(8,128)(2,1)S(1)}, u32[]{:S(2)}, u32[]{:S(2)}) collective-permute-start(bf16[384,192]{0,1:T(8,128)(2,1)S(1)} %collective-permute-done.4), channel_id=1, source_target_pairs={{0,508},{4,0},{8,4},{12,8},{16,12},{20,16},{24,20},{28,24},{32,28}... | collective-permute-start | bytes 442376 | tf_op jit(solution)/shard_map/ppermute | solution.py:14
  133.6 11.6 %collective-permute-start.6 = (bf16[384,192]{0,1:T(8,128)(2,1)S(1)}, bf16[384,192]{0,1:T(8,128)(2,1)S(1)}, u32[]{:S(2)}, u32[]{:S(2)}) collective-permute-start(bf16[384,192]{0,1:T(8,128)(2,1)S(1)} %collective-permute-done.5), channel_id=1, source_target_pairs={{0,508},{4,0},{8,4},{12,8},{16,12},{20,16},{24,20},{28,24},{32,28}... | collective-permute-start | bytes 442376 | tf_op jit(solution)/shard_map/ppermute | solution.py:14
  144.0 65.8 %copy-start.17 = (s32[1,192]{1,0:T(1,128)S(1)}, s32[1,192]{1,0:T(1,128)}, u32[]{:S(2)}) copy-start(s32[1,192]{1,0:T(1,128)} %param.13) | copy-start | bytes 2308
  146.1 191.9 %all-gather.2.cloned.1.call-start = ((), (), s32[]{:S(2)}) async-start(), calls=%async_computation.2 | async-start | bytes 1474560 | tf_op jit(solution)/shard_map/all_gather | solution.py:101
  204.3 6.7 %copy-start.6 = (bf16[384,192]{0,1:T(8,128)(2,1)S(1)}, bf16[384,192]{0,1:T(8,128)(2,1)}, u32[]{:S(2)}) copy-start(bf16[384,192]{0,1:T(8,128)(2,1)} %copy-done.5) | copy-start | bytes 442372
  204.3 6.7 %copy-start.8 = (bf16[192,192]{1,0:T(8,128)(2,1)S(1)}, bf16[192,192]{1,0:T(8,128)(2,1)}, u32[]{:S(2)}) copy-start(bf16[192,192]{1,0:T(8,128)(2,1)} %get-tuple-element.9) | copy-start | bytes 221188
  205.5 17.1 %collective-permute-start.7 = (f32[384,192]{0,1:T(8,128)S(1)}, f32[384,192]{0,1:T(8,128)S(1)}, u32[]{:S(2)}, u32[]{:S(2)}) collective-permute-start(f32[384,192]{0,1:T(8,128)S(1)} %fusion.19), channel_id=1, source_target_pairs={{0,4},{4,8},{8,12},{12,16},{16,20},{20,24},{24,28},{28,32},{32,36}... | collective-permute-start | bytes 884744 | tf_op jit(solution)/shard_map/ppermute | solution.py:14
  209.8 12.8 %copy-start.12 = (bf16[192,192]{1,0:T(8,128)(2,1)S(1)}, bf16[192,192]{1,0:T(8,128)(2,1)}, u32[]{:S(2)}) copy-start(bf16[192,192]{1,0:T(8,128)(2,1)} %get-tuple-element.4) | copy-start | bytes 221188
  211.0 13.8 %copy-start.13 = (bf16[192,192]{1,0:T(8,128)(2,1)S(1)}, bf16[192,192]{1,0:T(8,128)(2,1)}, u32[]{:S(2)}) copy-start(bf16[192,192]{1,0:T(8,128)(2,1)} %get-tuple-element.5) | copy-start | bytes 221188
  222.9 15.5 %collective-permute-start.8 = (f32[384,192]{0,1:T(8,128)S(1)}, f32[384,192]{0,1:T(8,128)S(1)}, u32[]{:S(2)}, u32[]{:S(2)}) collective-permute-start(f32[384,192]{0,1:T(8,128)S(1)} %convolution_add_fusion.7), channel_id=1, source_target_pairs={{0,4},{4,8},{8,12},{12,16},{16,20},{20,24},{24,28},{28,32},{32,36}... | collective-permute-start | bytes 884744 | tf_op jit(solution)/shard_map/ppermute | solution.py:14
  225.1 15.2 %copy-start.14 = (bf16[192,192]{1,0:T(8,128)(2,1)S(1)}, bf16[192,192]{1,0:T(8,128)(2,1)}, u32[]{:S(2)}) copy-start(bf16[192,192]{1,0:T(8,128)(2,1)} %get-tuple-element.6) | copy-start | bytes 221188
  225.4 15.3 %copy-start.15 = (bf16[192,192]{1,0:T(8,128)(2,1)S(1)}, bf16[192,192]{1,0:T(8,128)(2,1)}, u32[]{:S(2)}) copy-start(bf16[192,192]{1,0:T(8,128)(2,1)} %get-tuple-element.7) | copy-start | bytes 221188
  238.4 14.5 %collective-permute-start.9 = (f32[384,192]{0,1:T(8,128)S(1)}, f32[384,192]{0,1:T(8,128)S(1)}, u32[]{:S(2)}, u32[]{:S(2)}) collective-permute-start(f32[384,192]{0,1:T(8,128)S(1)} %add.201), channel_id=1, source_target_pairs={{0,4},{4,8},{8,12},{12,16},{16,20},{20,24},{24,28},{28,32},{32,36}... | collective-permute-start | bytes 884744 | tf_op jit(solution)/shard_map/ppermute | solution.py:14
  253.0 13.6 %collective-permute-start.10 = (f32[384,192]{0,1:T(8,128)S(1)}, f32[384,192]{0,1:T(8,128)S(1)}, u32[]{:S(2)}, u32[]{:S(2)}) collective-permute-start(f32[384,192]{0,1:T(8,128)S(1)} %add.202), channel_id=1, source_target_pairs={{0,4},{4,8},{8,12},{12,16},{16,20},{20,24},{24,28},{28,32},{32,36}... | collective-permute-start | bytes 884744 | tf_op jit(solution)/shard_map/ppermute | solution.py:14
  266.6 13.2 %collective-permute-start.11 = (f32[384,192]{0,1:T(8,128)S(1)}, f32[384,192]{0,1:T(8,128)S(1)}, u32[]{:S(2)}, u32[]{:S(2)}) collective-permute-start(f32[384,192]{0,1:T(8,128)S(1)} %add.203), channel_id=1, source_target_pairs={{0,4},{4,8},{8,12},{12,16},{16,20},{20,24},{24,28},{28,32},{32,36}... | collective-permute-start | bytes 884744 | tf_op jit(solution)/shard_map/ppermute | solution.py:14
  279.9 13.2 %collective-permute-start.12 = (f32[384,192]{0,1:T(8,128)S(1)}, f32[384,192]{0,1:T(8,128)S(1)}, u32[]{:S(2)}, u32[]{:S(2)}) collective-permute-start(f32[384,192]{0,1:T(8,128)S(1)} %add.204), channel_id=1, source_target_pairs={{0,4},{4,8},{8,12},{12,16},{16,20},{20,24},{24,28},{28,32},{32,36}... | collective-permute-start | bytes 884744 | tf_op jit(solution)/shard_map/ppermute | solution.py:14
  282.1 13.0 %copy-start.11 = (bf16[192,192]{1,0:T(8,128)(2,1)S(1)}, bf16[192,192]{1,0:T(8,128)(2,1)}, u32[]{:S(2)}) copy-start(bf16[192,192]{1,0:T(8,128)(2,1)} %get-tuple-element.3) | copy-start | bytes 221188
  282.3 13.0 %copy-start.10 = (bf16[192,192]{1,0:T(8,128)(2,1)S(1)}, bf16[192,192]{1,0:T(8,128)(2,1)}, u32[]{:S(2)}) copy-start(bf16[192,192]{1,0:T(8,128)(2,1)} %get-tuple-element.10) | copy-start | bytes 221188
  293.1 13.2 %collective-permute-start.13 = (f32[384,192]{0,1:T(8,128)S(1)}, f32[384,192]{0,1:T(8,128)S(1)}, u32[]{:S(2)}, u32[]{:S(2)}) collective-permute-start(f32[384,192]{0,1:T(8,128)S(1)} %add.205), channel_id=1, source_target_pairs={{0,4},{4,8},{8,12},{12,16},{16,20},{20,24},{24,28},{28,32},{32,36}... | collective-permute-start | bytes 884744 | tf_op jit(solution)/shard_map/ppermute | solution.py:14
  295.2 11.1 %copy-start.3 = (f32[384,1,192]{0,2,1:T(8,128)}, f32[384,1,192]{0,2,1:T(8,128)S(1)}, u32[]{:S(2)}) copy-start(f32[384,1,192]{0,2,1:T(8,128)S(1)} %fusion) | copy-start | bytes 884740
  295.3 11.1 %copy-start.1 = (f32[384,2,192]{0,2,1:T(8,128)S(1)}, f32[384,2,192]{0,2,1:T(8,128)}, u32[]{:S(2)}) copy-start(f32[384,2,192]{0,2,1:T(8,128)} %reduce-scatter.2.cloned.1.call-done) | copy-start | bytes 1769476
  319.0 5.8 %copy-start.9 = (bf16[192,192]{1,0:T(8,128)(2,1)S(1)}, bf16[192,192]{1,0:T(8,128)(2,1)}, u32[]{:S(2)}) copy-start(bf16[192,192]{1,0:T(8,128)(2,1)} %get-tuple-element.9) | copy-start | bytes 221188
  (3 other events, 6.2 us)
Sparse Core Ops, SparseCore 0:
  12.0 43.6 reduce-scatter.1
  146.2 58.0 all-reduce.2
  321.0 16.9 all-gather.1
where the time goes:
time: 349 us; the launch traced here: 348 us
  waiting for transfers between devices  201 us (58%)
  starting transfers between devices  82.9 us (24%)
  matrix products  18.3 us (5%)
  blocking collectives  17.8 us (5%)
  between operations  15.6 us (4%)
  other arithmetic  11.2 us (3%)
    ppermute x14, waiting for transfers between devices, from_behind(): lax.ppermute(value, axis, [(i, (i + by) % peers) for i in range(peers)])  88.2 us
    ppermute x14, starting transfers between devices, from_behind(): lax.ppermute(value, axis, [(i, (i + by) % peers) for i in range(peers)])  82.8 us
    psum x1, waiting for transfers between devices, shards(): lax.psum(partial_tile(partner).astype(jnp.bfloat16), 'mp')  56.8 us
    reduce_scatter x1, waiting for transfers between devices, shards(): lax.psum_scatter(jnp.stack([img_term, txt_term], axis=1), 'mp', scatter_d...  43.7 us
    psum x1, blocking collectives, shards(): radial_dots = lax.psum(jnp.sum(unit_vecs * step_pair, axis=0), 'mp')  12.4 us
    all_gather x1, waiting for transfers between devices, shards(): gathered = lax.all_gather(delta_rows, 'mp', axis=0, tiled=True)  12.2 us
  transfers between devices with their start and end apart: 17, of which 17 were waited for; matrix products, arithmetic and copies ran while one was open for 4% of the time, Pallas kernels for 0%

commit v1 on v0

v1 whole, which is shorter than its diff:
```python
import functools

import jax
import jax.numpy as jnp
from jax import lax
from jax.experimental import pallas as pl
from jax.experimental.pallas import tpu as pltpu
from jax.sharding import PartitionSpec as P

MESH = pl.DeviceIdType.MESH
STEPS = 8
VISITS = STEPS // 2
PARTS = 3
WIDE = 512

norm_eps = 1e-06
F32 = jnp.float32
BF16 = jnp.bfloat16

NN = (((1,), (0,)), ((), ()))
NT = (((1,), (1,)), ((), ()))


def mm(a, b, dims=NN):
    return lax.dot_general(a, b, dims, preferred_element_type=F32)


def kernel(
    n,
    xi_hbm, xt_hbm, wi_hbm, wt_hbm, scale_ref, shift_ref, partner_ref,
    gi_ref, gt_ref, loss_ref,
    x, w, psend, pown, precv, ysend, yrecv, unit, radius,
    a, b, slope, slope_t, da, rsend, rrecv,
    dbsend, dbown, dbrecv, y1send, y1recv, y0send, y0recv, xsend, xrecv,
    delta, lsend, lrecv, lstage, lpeer,
    load_sem, ss, rs,
):
    c = lax.axis_index("dp")
    m = lax.axis_index("mp")
    lo, k = m // 2, m % 2
    mq = (m + 2) % 4
    q = a.shape[0] // VISITS
    rows = 4 * q
    cols = w.shape[2]
    part = q // PARTS

    core = (c, m + 1 - 2 * k)
    near = (c, mq)
    prev = ((c + n - 1) % n, mq)
    after = ((c + 1) % n, mq)
    up = [((c + 2 * s) % n, m) for s in range(1, VISITS)]
    down = [((c + n - 2 * s) % n, m) for s in range(1, VISITS)]

    loads = []
    for i, (src, dst) in enumerate(
        [(xi_hbm, x.at[0]), (wi_hbm, w.at[0]), (xt_hbm, x.at[1]), (wt_hbm, w.at[1])]
    ):
        load = pltpu.make_async_copy(src, dst, load_sem.at[i])
        load.start()
        loads.append(load)

    barrier = pltpu.get_barrier_semaphore()
    peers = [core, near, prev, after] + up + [down[0]]
    for peer in peers:
        pl.semaphore_signal(barrier, inc=1, device_id=peer, device_id_type=MESH)

    count = [0]
    sent = []

    def message(src, dst, target):
        i = count[0]
        count[0] += 1
        return pltpu.make_async_remote_copy(
            src_ref=src, dst_ref=dst, send_sem=ss.at[i], recv_sem=rs.at[i],
            device_id=target, device_id_type=MESH,
        )

    def send(copy):
        copy.start()
        sent.append(copy)
        return copy

    def at(start, size):
        return pl.ds(pl.multiple_of(start, 16), size)

    def quarter(j):
        return at(j * q, q)

    def piece(j):
        return pl.ds(j * part, part)

    def spans():
        return [slice(i, i + WIDE) for i in range(0, cols, WIDE)]

    def project(t, which, out, to):
        left = jnp.concatenate([x[t, quarter(which), :], x[t, quarter(which + 2), :]], axis=0)
        for span in spans():
            out[t, :, span] = mm(left, w[t, :, span]).astype(to)

    first = []
    for t in range(2):
        loads[2 * t].wait()
        loads[2 * t + 1].wait()
        project(t, 1 - k, psend, BF16)
        if t == 0:
            pl.semaphore_wait(barrier, len(peers))
        first.append(send(message(psend.at[t], precv.at[t], core)))
        project(t, k, pown, F32)

    second = []
    for t in range(2):
        first[t].wait_recv()
        ysend[t] = (
            pown[t, quarter(1 - lo), :] + precv[t, quarter(1 - lo), :].astype(F32)
        ).astype(BF16)
        second.append(send(message(ysend.at[t], yrecv.at[t], near)))

    def normalise(t):
        raw = (
            pown[t, quarter(lo), :]
            + precv[t, quarter(lo), :].astype(F32)
            + yrecv[t].astype(F32)
        )
        size = jnp.sqrt(jnp.sum(raw * raw, axis=1, keepdims=True) + norm_eps)
        value = raw / size
        unit[t] = value
        radius[t] = jnp.broadcast_to(size, radius.shape[1:])
        return value.astype(BF16)

    second[0].wait_recv()
    a[0:q] = normalise(0)

    def visit(s, j):
        return message(
            a.at[pl.ds(s * q + j * part, part)], a.at[pl.ds((s + 1) * q + j * part, part)], up[0]
        )

    hops = [[visit(s, j) for j in range(PARTS)] for s in range(VISITS - 1)]
    for hop in hops[0]:
        send(hop)

    second[1].wait_recv()
    b[quarter(m)] = normalise(1)

    def text(block, j, into, target, size=q, skip=0):
        return message(
            b.at[at(block * rows + j * q + skip, size)],
            b.at[at(into * rows + j * q + skip, size)],
            target,
        )

    across = [send(text(0, m, 1, prev, part, j * part)) for j in range(PARTS)]
    beside = [send(text(0, m, 0, near, part, j * part)) for j in range(PARTS)]
    in_chip = [send(text(0, m, 0, core))]

    for j in range(PARTS):
        hops[0][j].wait_recv()
        send(hops[1][j])

    relay = []
    for j in range(PARTS):
        across[j].wait_recv()
        relay.append(send(text(1, mq, 1, near, part, j * part)))
    in_chip.append(send(text(1, mq, 1, core)))
    for j in range(PARTS):
        beside[j].wait_recv()
    in_chip.append(send(text(0, mq, 0, core)))
    for j in range(PARTS):
        hops[1][j].wait_recv()
        send(hops[2][j])
    for j in range(PARTS):
        relay[j].wait_recv()
    in_chip.append(send(text(1, m, 1, core)))
    for copy in in_chip:
        copy.wait_recv()
    for j in range(PARTS):
        hops[2][j].wait_recv()

    temperature = jnp.exp(jnp.full((q, 2 * rows), scale_ref[0], F32))
    shift = shift_ref[0]
    named = (
        lax.broadcasted_iota(jnp.int32, (2 * rows, rows), 0) == partner_ref[...]
    ).astype(BF16)
    own = (
        lax.broadcasted_iota(jnp.int32, (q, rows), 1)
        == lax.broadcasted_iota(jnp.int32, (q, rows), 0) + m * q
    )
    positive = mm(own.astype(BF16), named, NT) > 0.5
    scores = mm(a[...], b[...], NT)
    losses = []
    for s in range(VISITS):
        logits = temperature * scores[s * q:(s + 1) * q] + shift
        z = jnp.where(positive, -logits, logits) if s == 0 else logits
        u = jnp.exp(-jnp.abs(z))
        soft = jnp.maximum(z, 0.0) + jnp.log1p(u)
        sig = jnp.where(z >= 0.0, 1.0, u) / (1.0 + u)
        grade = temperature * sig
        if s == 0:
            grade = jnp.where(positive, -grade, grade)
        slope[s * q:(s + 1) * q] = grade.astype(BF16)
        slope_t[:, s * q:(s + 1) * q] = grade.T.astype(BF16)
        losses.append(jnp.sum(soft, axis=1, keepdims=True))

    last = VISITS - 1
    far = slope[last * q:]
    for span in spans():
        rsend[last - 1, :, span] = mm(far, b[:, span]).astype(BF16)

    def homeward(s, j):
        return message(rsend.at[s - 1, piece(j)], rrecv.at[s - 1, piece(j)], down[0])

    ways = {s: [homeward(s, j) for j in range(PARTS)] for s in range(1, VISITS)}
    for way in ways[last]:
        send(way)

    def text_side(which):
        return jnp.concatenate([slope_t[at(i * 2 * q + which * q, q)] for i in range(4)], axis=0)

    left = text_side(1 - k)
    for span in spans():
        dbsend[:, span] = mm(left, a[:, span]).astype(BF16)
    swap = send(message(dbsend, dbrecv, core))
    left = text_side(k)
    for span in spans():
        dbown[:, span] = mm(left, a[:, span])
    for span in spans():
        da[:, span] = mm(slope[:last * q], b[:, span])

    spread = (
        lax.broadcasted_iota(jnp.int32, (q, lsend.shape[2]), 1)
        == lax.broadcasted_iota(jnp.int32, (q, lsend.shape[2]), 0) + m * q
    )

    def as_lanes(column):
        line = jnp.sum(jnp.where(spread, column, 0.0), axis=0, keepdims=True)
        return jnp.broadcast_to(line, lsend.shape[1:])

    home = []
    for s in range(1, VISITS):
        lsend[s - 1] = as_lanes(losses[s])
        home.append(send(message(lsend.at[s - 1], lrecv.at[s - 1], down[s - 1])))

    swap.wait_recv()

    def chip_sum(block, half):
        where = at((2 * block + half) * q, q)
        return dbown[where] + dbrecv[where].astype(F32)

    y1send[...] = chip_sum(1, lo).astype(BF16)
    beside1 = [
        send(message(y1send.at[piece(j)], y1recv.at[piece(j)], near)) for j in range(PARTS)
    ]
    y0send[...] = chip_sum(0, 1 - lo).astype(BF16)
    beside0 = send(message(y0send, y0recv, near))

    def add_way(s, j):
        ways[s + 1][j].wait_recv()
        at_home = pl.ds(s * q + j * part, part)
        total = da[at_home] + rrecv[s, piece(j)].astype(F32)
        return total

    for j in range(PARTS):
        rsend[1, piece(j)] = add_way(2, j).astype(BF16)
        send(ways[2][j])

    over = []
    for j in range(PARTS):
        beside1[j].wait_recv()
        where = at((2 + 1 - lo) * q + j * part, part)
        xsend[piece(j)] = (
            dbown[where] + dbrecv[where].astype(F32) + y1recv[piece(j)].astype(F32)
        ).astype(BF16)
        over.append(send(message(xsend.at[piece(j)], xrecv.at[piece(j)], after)))

    total = as_lanes(losses[0])
    for s in range(1, VISITS):
        home[s - 1].wait_recv()
        total = total + lrecv[s - 1]
    lstage[0] = total
    pair = send(message(lstage.at[0], lpeer.at[0], core))

    for j in range(PARTS):
        rsend[0, piece(j)] = add_way(1, j).astype(BF16)
        send(ways[1][j])

    pair.wait_recv()
    lstage[1] = lstage[0] + lpeer[0]
    pair = send(message(lstage.at[1], lpeer.at[1], near))

    def tangent(t, step, where):
        vec = unit[t, where]
        radial = jnp.sum(vec * step, axis=1, keepdims=True)
        return ((step - vec * radial) / radius[t, where, 0:1]).astype(BF16)

    def gather(t, j, target, size=q, skip=0):
        where = at(j * q + skip, size)
        return message(delta.at[t, where], delta.at[t, where], target)

    beside0.wait_recv()
    for copy in over:
        copy.wait_recv()
    step = chip_sum(0, lo) + y0recv[...].astype(F32) + xrecv[...].astype(F32)
    delta[1, quarter(m)] = tangent(1, step, slice(0, q))
    text_near = send(gather(1, m, near))
    text_core = [send(gather(1, m, core))]

    image_near = []
    for j in range(PARTS):
        step = add_way(0, j)
        delta[0, at(m * q + j * part, part)] = tangent(0, step, piece(j))
        image_near.append(send(gather(0, m, near, part, j * part)))
    image_core = [send(gather(0, m, core))]

    text_near.wait_recv()
    text_core.append(send(gather(1, mq, core)))
    pair.wait_recv()
    loss = (lstage[1] + lpeer[1]) * (1.0 / (STEPS * rows))
    loss_ref[...] = loss[0:1, 0:rows]
    for copy in text_core:
        copy.wait_recv()
    gt_ref[...] = mm(delta[1], w[1], NT).astype(BF16)

    for copy in image_near:
        copy.wait_recv()
    image_core.append(send(gather(0, mq, core)))
    for copy in image_core:
        copy.wait_recv()
    gi_ref[...] = mm(delta[0], w[0], NT).astype(BF16)

    for copy in sent:
        copy.wait_send()


def shards(n, xi, xt, wi, wt, scale, shift, partner):
    rows, share = xi.shape
    cols = wi.shape[1]
    q = rows // 4
    vm = pltpu.VMEM
    lanes = -(-rows // 128) * 128
    messages = 64
    gi, gt, loss = pl.pallas_call(
        functools.partial(kernel, n),
        out_shape=(
            jax.ShapeDtypeStruct((rows, share), BF16),
            jax.ShapeDtypeStruct((rows, share), BF16),
            jax.ShapeDtypeStruct((1, rows), F32),
        ),
        in_specs=[pl.BlockSpec(memory_space=pl.ANY)] * 4
        + [pl.BlockSpec(memory_space=pltpu.SMEM)] * 2
        + [pl.BlockSpec(memory_space=pltpu.VMEM)],
        out_specs=(pl.BlockSpec(memory_space=pltpu.VMEM),) * 3,
        scratch_shapes=[
            vm((2, rows, share), BF16),
            vm((2, share, cols), BF16),
            vm((2, 2 * q, cols), BF16),
            vm((2, 2 * q, cols), F32),
            vm((2, 2 * q, cols), BF16),
            vm((2, q, cols), BF16),
            vm((2, q, cols), BF16),
            vm((2, q, cols), F32),
            vm((2, q, 128), F32),
            vm((VISITS * q, cols), BF16),
            vm((2 * rows, cols), BF16),
            vm((VISITS * q, 2 * rows), BF16),
            vm((2 * rows, VISITS * q), BF16),
            vm(((VISITS - 1) * q, cols), F32),
            vm((VISITS - 1, q, cols), BF16),
            vm((VISITS - 1, q, cols), BF16),
            vm((4 * q, cols), BF16),
            vm((4 * q, cols), F32),
            vm((4 * q, cols), BF16),
            vm((q, cols), BF16),
            vm((q, cols), BF16),
            vm((q, cols), BF16),
            vm((q, cols), BF16),
            vm((q, cols), BF16),
            vm((q, cols), BF16),
            vm((2, rows, cols), BF16),
            vm((VISITS - 1, 8, lanes), F32),
            vm((VISITS - 1, 8, lanes), F32),
            vm((2, 8, lanes), F32),
            vm((2, 8, lanes), F32),
            pltpu.SemaphoreType.DMA((4,)),
            pltpu.SemaphoreType.DMA((messages,)),
            pltpu.SemaphoreType.DMA((messages,)),
        ],
        compiler_params=pltpu.CompilerParams(
            collective_id=0, has_side_effects=True, vmem_limit_bytes=48 * 2**20
        ),
    )(xi, xt, wi, wt, scale, shift, partner)
    return gi, gt, loss.reshape(rows)


def solution(mesh):
    placed = (P("dp", "mp"), P("dp", "mp"), P("mp", None), P("mp", None), P(), P(), P("dp", None))
    return jax.shard_map(
        functools.partial(shards, mesh.shape["dp"]),
        mesh=mesh,
        in_specs=placed,
        out_specs=(P("dp", "mp"), P("dp", "mp"), P("dp")),
        check_vma=False,
    )
```

time: 349 us -> 72.1 us (0.21)
  waiting for transfers between devices: 201 us -> 0 us
  starting transfers between devices: 82.9 us -> 0 us
  Pallas kernels: 0 us -> 62.9 us
  matrix products: 18.3 us -> 0 us
  blocking collectives: 17.8 us -> 0 us
  between operations: 15.6 us -> 1.95 us
  other arithmetic: 11.2 us -> 0 us
  local copies, waits for them, and re-layouts: 1.31 us -> 6.92 us
    ppermute x14 -> x0, waiting for transfers between devices: 88.2 us -> none  [from_behind(): lax.ppermute(value, axis, [(i, (i + by) % peers) for i in range(peers)])]
    ppermute x14 -> x0, starting transfers between devices: 82.8 us -> none  [from_behind(): lax.ppermute(value, axis, [(i, (i + by) % peers) for i in range(peers)])]
    pallas_call x0 -> x1, Pallas kernels: none -> 62.9 us  [shards(): pl.pallas_call(functools.partial(kernel, n), out_shape=(jax.ShapeDtypeStr...]
    psum x1 -> x0, waiting for transfers between devices: 56.8 us -> none  [shards(): lax.psum(partial_tile(partner).astype(jnp.bfloat16), 'mp')]
    reduce_scatter x1 -> x0, waiting for transfers between devices: 43.7 us -> none  [shards(): lax.psum_scatter(jnp.stack([img_term, txt_term], axis=1), 'mp', scatter_d...]
    dot_general x28 -> x0, matrix products: 18.3 us -> none  [the longest x8 6.92 us: partial_tile(): lax.dot_general(img_emb, partner, (((0,), (0,)), ((), ())), preferred_ele...]
    psum x2 -> x0, blocking collectives: 17.8 us -> none  [the longest x1 12.4 us: shards(): radial_dots = lax.psum(jnp.sum(unit_vecs * step_pair, axis=0), 'mp')]
    all_gather x1 -> x0, waiting for transfers between devices: 12.2 us -> none  [shards(): gathered = lax.all_gather(delta_rows, 'mp', axis=0, tiled=True)]
  transfers between devices with their start and end apart: 17 -> 0, of which waited for: 17 -> 0; matrix products, arithmetic and copies ran while one was open for 4% -> 0% of each run, Pallas kernels for 0% -> 0%
where the time goes in v1:
time: 72.1 us; the launch traced here: 71.8 us
  Pallas kernels  62.9 us (87%)
  local copies, waits for them, and re-layouts  6.92 us (10%)
  between operations  1.95 us (3%)
    pallas_call x1, Pallas kernels, shards(): pl.pallas_call(functools.partial(kernel, n), out_shape=(jax.ShapeDtypeStr...  62.9 us
    unnamed x13, local copies, waits for them, and re-layouts  6.92 us

profile of v1, /device:TPU:1, one launch (start us, length us, event | category | flops | bytes accessed | tf_op | source)
XLA Modules:
  0.0 71.8 jit_solution(13365743798808750129)
XLA Ops:
  1.9 0.0 copy-start
  1.9 1.3 %copy-done = bf16[384,1536]{1,0:T(8,128)(2,1)S(1)} copy-done((bf16[384,1536]{1,0:T(8,128)(2,1)S(1)}, bf16[384,1536]{1,0:T(8,128)(2,1)}, u32[]{:S(2)}) %copy-start) | copy-done | bytes 1179672
  3.2 0.0 copy-start.1
  3.2 1.3 %copy-done.1 = bf16[384,1536]{1,0:T(8,128)(2,1)S(1)} copy-done((bf16[384,1536]{1,0:T(8,128)(2,1)S(1)}, bf16[384,1536]{1,0:T(8,128)(2,1)}, u32[]{:S(2)}) %copy-start.1) | copy-done | bytes 1179672
  4.5 0.0 copy-start.2
  4.5 0.9 %copy-done.2 = bf16[192,384]{1,0:T(8,128)(2,1)S(1)} copy-done((bf16[192,384]{1,0:T(8,128)(2,1)S(1)}, bf16[192,384]{1,0:T(8,128)(2,1)}, u32[]{:S(2)}) %copy-start.2) | copy-done | bytes 147480
  5.4 0.0 copy-start.3
  5.4 0.9 %copy-done.3 = bf16[192,384]{1,0:T(8,128)(2,1)S(1)} copy-done((bf16[192,384]{1,0:T(8,128)(2,1)S(1)}, bf16[192,384]{1,0:T(8,128)(2,1)}, u32[]{:S(2)}) %copy-start.3) | copy-done | bytes 147480
  6.3 0.0 copy-start.4
  6.3 0.7 copy-done.4
  7.0 62.9 %shard_map.94 = (bf16[192,384]{1,0:T(8,128)(2,1)S(1)}, bf16[192,384]{1,0:T(8,128)(2,1)S(1)}, f32[1,192]{1,0:T(1,128)S(1)}) custom-call(bf16[192,384]{1,0:T(8,128)(2,1)S(1)} %copy-done.2, bf16[192,384]{1,0:T(8,128)(2,1)S(1)} %copy-done.3, bf16[384,1536]{1,0:T(8,128)(2,1)S(1)} %copy-done, bf16[384,1536]{1,0:T(8,128)(2,1)S(1)} %copy-done.1, ...), custom_call_target="tpu_custom_call" | custom-call | tf_op jit(solution)/shard_map/pallas_call | solution.py:341
  69.9 0.7 copy.15
  70.6 0.7 copy.16
  71.2 0.6 copy.17
Async XLA Ops:
  1.9 1.3 %copy-start = (bf16[384,1536]{1,0:T(8,128)(2,1)S(1)}, bf16[384,1536]{1,0:T(8,128)(2,1)}, u32[]{:S(2)}) copy-start(bf16[384,1536]{1,0:T(8,128)(2,1)} %wi_hbm.1) | copy-start | bytes 3538948
  3.2 1.3 %copy-start.1 = (bf16[384,1536]{1,0:T(8,128)(2,1)S(1)}, bf16[384,1536]{1,0:T(8,128)(2,1)}, u32[]{:S(2)}) copy-start(bf16[384,1536]{1,0:T(8,128)(2,1)} %wt_hbm.1) | copy-start | bytes 3538948
  4.5 0.9 %copy-start.2 = (bf16[192,384]{1,0:T(8,128)(2,1)S(1)}, bf16[192,384]{1,0:T(8,128)(2,1)}, u32[]{:S(2)}) copy-start(bf16[192,384]{1,0:T(8,128)(2,1)} %xi_hbm.1) | copy-start | bytes 442372
  5.4 0.9 %copy-start.3 = (bf16[192,384]{1,0:T(8,128)(2,1)S(1)}, bf16[192,384]{1,0:T(8,128)(2,1)}, u32[]{:S(2)}) copy-start(bf16[192,384]{1,0:T(8,128)(2,1)} %xt_hbm.1) | copy-start | bytes 442372
  6.3 0.7 copy-start.4

commit v2 on v1

v2 whole, which is shorter than its diff:
```python
import functools

import jax
import jax.numpy as jnp
from jax import lax
from jax.experimental import pallas as pl
from jax.experimental.pallas import tpu as pltpu
from jax.sharding import PartitionSpec as P

MESH = pl.DeviceIdType.MESH
STEPS = 8
VISITS = STEPS // 2
PARTS = 3
WIDE = 512

norm_eps = 1e-06
F32 = jnp.float32
BF16 = jnp.bfloat16

NN = (((1,), (0,)), ((), ()))
NT = (((1,), (1,)), ((), ()))


def mm(a, b, dims=NN):
    return lax.dot_general(a, b, dims, preferred_element_type=F32)


def spans(cols):
    return [slice(i, i + WIDE) for i in range(0, cols, WIDE)]


def kernel(
    n,
    xi_hbm, xt_hbm, wi_hbm, wt_hbm, scale_hbm, shift_hbm, partner_hbm,
    gi_hbm, gt_hbm, loss_hbm,
    gi_ref, gt_ref, loss_ref, x, w, partner_ref, scale_ref, shift_ref, psend, pown, precv, ysend, yrecv, unit, radius,
    a, b, slope, slope_t, da, rsend, rrecv,
    dbsend, dbown, dbrecv, y1send, y1recv, y0send, y0recv, xsend, xrecv,
    delta, lsend, lrecv, lstage, lpeer,
    load_sem, out_sem, ss, rs,
):
    c = lax.axis_index("dp")
    m = lax.axis_index("mp")
    lo, k = m // 2, m % 2
    mq = (m + 2) % 4
    q = a.shape[0] // VISITS
    rows = 4 * q
    cols = w.shape[2]
    part = q // PARTS

    core = (c, m + 1 - 2 * k)
    near = (c, mq)
    prev = ((c + n - 1) % n, mq)
    after = ((c + 1) % n, mq)
    up = ((c + 2) % n, m)
    down = [((c + n - 2 * s) % n, m) for s in range(1, VISITS)]

    loads = {}
    for i, (name, src, dst) in enumerate(
        [("x0", xi_hbm, x.at[0])]
        + [(f"w0{j}", wi_hbm.at[:, span], w.at[0, :, span]) for j, span in enumerate(spans(cols))]
        + [("x1", xt_hbm, x.at[1])]
        + [(f"w1{j}", wt_hbm.at[:, span], w.at[1, :, span]) for j, span in enumerate(spans(cols))]
        + [("p", partner_hbm, partner_ref), ("t", scale_hbm, scale_ref), ("b", shift_hbm, shift_ref)]
    ):
        loads[name] = pltpu.make_async_copy(src, dst, load_sem.at[i])
        loads[name].start()

    barrier = pltpu.get_barrier_semaphore()
    peers = [core, near, prev, after, up, down[0]]
    for peer in peers:
        pl.semaphore_signal(barrier, inc=1, device_id=peer, device_id_type=MESH)

    count = [0]
    sent = []

    def message(src, dst, target):
        i = count[0]
        count[0] += 1
        return pltpu.make_async_remote_copy(
            src_ref=src, dst_ref=dst, send_sem=ss.at[i], recv_sem=rs.at[i],
            device_id=target, device_id_type=MESH,
        )

    def send(copy):
        copy.start()
        sent.append(copy)
        return copy

    def drain():
        for copy in sent:
            copy.wait_send()
        sent.clear()

    def at(start, size):
        return pl.ds(pl.multiple_of(start, 16), size)

    def piece(j, base=0):
        return pl.ds(base + j * part, part)

    pieces = range(PARTS)

    def project(t, chip, which, out, to, ready=False):
        left = x[t, at((2 * chip + which) * q, q), :]
        for j, span in enumerate(spans(cols)):
            if not ready:
                loads[f"w{t}{j}"].wait()
            out[:, span] = mm(left, w[t, :, span]).astype(to)

    first = [[None, None], [None, None]]
    for t in range(2):
        loads[f"x{t}"].wait()
        project(t, 1 - lo, 1 - k, psend.at[t, 0], BF16)
        if t == 0:
            pl.semaphore_wait(barrier, len(peers))
        first[t][0] = send(message(psend.at[t, 0], precv.at[t, 0], core))
    for t in range(2):
        project(t, 1 - lo, k, pown.at[t, 0], F32, True)
    project(0, lo, 1 - k, psend.at[0, 1], BF16, True)
    first[0][1] = send(message(psend.at[0, 1], precv.at[0, 1], core))

    second = [[], []]

    def over_y(t):
        first[t][0].wait_recv()
        for j in pieces:
            here = piece(j)
            ysend[t, here] = (pown[t, 0, here] + precv[t, 0, here].astype(F32)).astype(BF16)
            second[t].append(send(message(ysend.at[t, here], yrecv.at[t, here], near)))

    over_y(0)
    over_y(1)
    project(1, lo, 1 - k, psend.at[1, 1], BF16, True)
    first[1][1] = send(message(psend.at[1, 1], precv.at[1, 1], core))
    for t in range(2):
        project(t, lo, k, pown.at[t, 1], F32, True)

    def normalise(t, j):
        here = piece(j)
        second[t][j].wait_recv()
        raw = pown[t, 1, here] + precv[t, 1, here].astype(F32) + yrecv[t, here].astype(F32)
        size = jnp.sqrt(jnp.sum(raw * raw, axis=1, keepdims=True) + norm_eps)
        value = raw / size
        unit[t, here] = value
        radius[t, here] = jnp.broadcast_to(size, (part, radius.shape[2]))
        return value.astype(BF16)

    def visit(s, j):
        return message(a.at[piece(j, s * q)], a.at[piece(j, (s + 1) * q)], up)

    def text(into, j, target, size=q, skip=0, block=None):
        block = into if block is None else block
        return message(
            b.at[at(block * rows + j * q + skip, size)],
            b.at[at(into * rows + j * q + skip, size)],
            target,
        )

    hops = [[visit(s, j) for j in pieces] for s in range(VISITS - 1)]
    first[0][1].wait_recv()
    for j in pieces:
        a[piece(j)] = normalise(0, j)
        send(hops[0][j])

    first[1][1].wait_recv()
    across, beside, relay, in_chip = [], [], [], []
    for j in pieces:
        b[at(m * q + j * part, part)] = normalise(1, j)
        across.append(send(text(1, m, prev, part, j * part, block=0)))
        beside.append(send(text(0, m, near, part, j * part)))
        hops[0][j].wait_recv()
        send(hops[1][j])
    in_chip.append(send(text(0, m, core)))
    for j in pieces:
        across[j].wait_recv()
        relay.append(send(text(1, mq, near, part, j * part)))
        hops[1][j].wait_recv()
        send(hops[2][j])
    in_chip.append(send(text(1, mq, core)))
    for j in pieces:
        beside[j].wait_recv()
    in_chip.append(send(text(0, mq, core)))

    for name in "ptb":
        loads[name].wait()
    temperature = jnp.exp(jnp.full((q, 2 * rows), scale_ref[0], F32))
    shift = shift_ref[0]
    named = (
        lax.broadcasted_iota(jnp.int32, (2 * rows, rows), 0) == partner_ref[...]
    ).astype(BF16)
    own = (
        lax.broadcasted_iota(jnp.int32, (q, rows), 1)
        == lax.broadcasted_iota(jnp.int32, (q, rows), 0) + m * q
    )
    positive = mm(own.astype(BF16), named, NT) > 0.5
    drain()

    for j in pieces:
        relay[j].wait_recv()
        in_chip.append(send(text(1, m, core, part, j * part)))
    for j in pieces:
        hops[2][j].wait_recv()
    for copy in in_chip:
        copy.wait_recv()

    losses = {}
    last = VISITS - 1

    def score(s, scores):
        logits = temperature * scores + shift
        z = jnp.where(positive, -logits, logits) if s == 0 else logits
        u = jnp.exp(-jnp.abs(z))
        soft = jnp.maximum(z, 0.0) + jnp.log1p(u)
        sig = jnp.where(z >= 0.0, 1.0, u) / (1.0 + u)
        grade = temperature * sig
        if s == 0:
            grade = jnp.where(positive, -grade, grade)
        slope[s * q:(s + 1) * q] = grade.astype(BF16)
        slope_t[:, s * q:(s + 1) * q] = grade.T.astype(BF16)
        losses[s] = jnp.sum(soft, axis=1, keepdims=True)

    scores = mm(a[...], b[...], NT)
    score(last, scores[last * q:])

    far = slope[last * q:]
    for span in spans(cols):
        rsend[last - 1, :, span] = mm(far, b[:, span]).astype(BF16)

    def homeward(s, j):
        return message(rsend.at[s - 1, piece(j)], rrecv.at[s - 1, piece(j)], down[0])

    ways = {s: [homeward(s, j) for j in pieces] for s in range(1, VISITS)}
    for way in ways[last]:
        send(way)
    for s in range(last):
        score(s, scores[s * q:(s + 1) * q])

    def text_side(block, which):
        return jnp.concatenate(
            [slope_t[at((2 * block + half) * 2 * q + which * q, q)] for half in range(2)], axis=0
        )

    swap = {}
    for block in (1, 0):
        left = text_side(block, 1 - k)
        for span in spans(cols):
            dbsend[block, :, span] = mm(left, a[:, span]).astype(BF16)
        swap[block] = send(message(dbsend.at[block], dbrecv.at[block], core))
    for block in (1, 0):
        left = text_side(block, k)
        for span in spans(cols):
            dbown[block, :, span] = mm(left, a[:, span])

    def chip_sum(block, half, j):
        where = at(half * q + j * part, part)
        return dbown[block, where] + dbrecv[block, where].astype(F32)

    beside1, beside0, over = [], [], []
    swap[1].wait_recv()
    for j in pieces:
        y1send[piece(j)] = chip_sum(1, lo, j).astype(BF16)
        beside1.append(send(message(y1send.at[piece(j)], y1recv.at[piece(j)], near)))
    for span in spans(cols):
        da[:, span] = mm(slope[:last * q], b[:, span])
    swap[0].wait_recv()
    for j in pieces:
        y0send[piece(j)] = chip_sum(0, 1 - lo, j).astype(BF16)
        beside0.append(send(message(y0send.at[piece(j)], y0recv.at[piece(j)], near)))

    def add_way(s, j):
        ways[s + 1][j].wait_recv()
        return da[piece(j, s * q)] + rrecv[s, piece(j)].astype(F32)

    def onward(s, j):
        rsend[s - 1, piece(j)] = add_way(s, j).astype(BF16)
        send(ways[s][j])

    def cross(j):
        beside1[j].wait_recv()
        xsend[piece(j)] = (chip_sum(1, 1 - lo, j) + y1recv[piece(j)].astype(F32)).astype(BF16)
        over.append(send(message(xsend.at[piece(j)], xrecv.at[piece(j)], after)))

    spread = (
        lax.broadcasted_iota(jnp.int32, (q, lsend.shape[2]), 1)
        == lax.broadcasted_iota(jnp.int32, (q, lsend.shape[2]), 0) + m * q
    )

    def as_lanes(column):
        line = jnp.sum(jnp.where(spread, column, 0.0), axis=0, keepdims=True)
        return jnp.broadcast_to(line, lsend.shape[1:])

    for j in pieces:
        onward(2, j)
    home = []
    for s in range(1, VISITS):
        lsend[s - 1] = as_lanes(losses[s])
        home.append(send(message(lsend.at[s - 1], lrecv.at[s - 1], down[s - 1])))
    for j in pieces:
        cross(j)
        onward(1, j)

    total = as_lanes(losses[0])
    for s in range(1, VISITS):
        home[s - 1].wait_recv()
        total = total + lrecv[s - 1]
    lstage[0] = total
    pair = send(message(lstage.at[0], lpeer.at[0], core))

    def tangent(t, step, j):
        here = piece(j)
        vec = unit[t, here]
        radial = jnp.sum(vec * step, axis=1, keepdims=True)
        return ((step - vec * radial) / radius[t, here, 0:1]).astype(BF16)

    def gather(t, j, target, size=q, skip=0):
        where = at(j * q + skip, size)
        return message(delta.at[t, where], delta.at[t, where], target)

    beyond = [[], []]
    inside = [[], []]

    def text_step(j):
        beside0[j].wait_recv()
        over[j].wait_recv()
        step = chip_sum(0, lo, j) + y0recv[piece(j)].astype(F32) + xrecv[piece(j)].astype(F32)
        delta[1, at(m * q + j * part, part)] = tangent(1, step, j)
        beyond[1].append(send(gather(1, m, near, part, j * part)))

    def image_step(j):
        delta[0, at(m * q + j * part, part)] = tangent(0, add_way(0, j), j)
        beyond[0].append(send(gather(0, m, near, part, j * part)))

    for j in pieces:
        text_step(j)
        image_step(j)
    for t in (1, 0):
        inside[t].append(send(gather(t, m, core)))

    pair.wait_recv()
    lstage[1] = lstage[0] + lpeer[0]
    pair = send(message(lstage.at[1], lpeer.at[1], near))
    drain()

    half = 2 * q

    def result(t, out, chip):
        where = at(chip * half, half)
        out[where] = mm(delta[t, where], w[t], NT).astype(BF16)

    for t in (1, 0):
        inside[t][0].wait_recv()
    result(1, gt_ref, lo)
    result(0, gi_ref, lo)
    for j in pieces:
        for t in (1, 0):
            beyond[t][j].wait_recv()
            inside[t].append(send(gather(t, mq, core, part, j * part)))
    pair.wait_recv()
    loss = (lstage[1] + lpeer[1]) * (1.0 / (STEPS * rows))
    loss_ref[...] = loss[0, 0:rows]
    stores = []

    def put(src, dst):
        copy = pltpu.make_async_copy(src, dst, out_sem.at[len(stores)])
        copy.start()
        stores.append(copy)

    put(loss_ref, loss_hbm)
    for t, out, out_hbm in ((1, gt_ref, gt_hbm), (0, gi_ref, gi_hbm)):
        for copy in inside[t][1:]:
            copy.wait_recv()
        result(t, out, 1 - lo)
        put(out, out_hbm)
    drain()
    for copy in stores:
        copy.wait()


def store(gi, gt, loss, gi_out, gt_out, loss_out, gi_held, gt_held, loss_held, sem):
    held = (gi_held, gt_held, loss_held)
    ins = [pltpu.make_async_copy(s, d, sem.at[i]) for i, (s, d) in enumerate(zip((gi, gt, loss), held))]
    outs = [
        pltpu.make_async_copy(s, d, sem.at[3 + i])
        for i, (s, d) in enumerate(zip(held, (gi_out, gt_out, loss_out)))
    ]
    for copy in ins:
        copy.start()
    for into, out in zip(ins, outs):
        into.wait()
        out.start()
    for out in outs:
        out.wait()


def shards(n, xi, xt, wi, wt, scale, shift, partner):
    rows, share = xi.shape
    cols = wi.shape[1]
    q = rows // 4
    vm = pltpu.VMEM
    lanes = -(-rows // 128) * 128
    messages = 128
    gi, gt, loss = pl.pallas_call(
        functools.partial(kernel, n),
        out_shape=(
            jax.ShapeDtypeStruct((rows, share), BF16),
            jax.ShapeDtypeStruct((rows, share), BF16),
            jax.ShapeDtypeStruct((rows,), F32),
        ),
        in_specs=[pl.BlockSpec(memory_space=pl.ANY)] * 7,
        out_specs=(pl.BlockSpec(memory_space=pl.ANY),) * 3,
        scratch_shapes=[
            vm((rows, share), BF16),
            vm((rows, share), BF16),
            vm((rows,), F32),
            vm((2, rows, share), BF16),
            vm((2, share, cols), BF16),
            vm((1, rows), jnp.int32),
            pltpu.SMEM((1,), F32),
            pltpu.SMEM((1,), F32),
            vm((2, 2, q, cols), BF16),
            vm((2, 2, q, cols), F32),
            vm((2, 2, q, cols), BF16),
            vm((2, q, cols), BF16),
            vm((2, q, cols), BF16),
            vm((2, q, cols), F32),
            vm((2, q, 128), F32),
            vm((VISITS * q, cols), BF16),
            vm((2 * rows, cols), BF16),
            vm((VISITS * q, 2 * rows), BF16),
            vm((2 * rows, VISITS * q), BF16),
            vm(((VISITS - 1) * q, cols), F32),
            vm((VISITS - 1, q, cols), BF16),
            vm((VISITS - 1, q, cols), BF16),
            vm((2, 2 * q, cols), BF16),
            vm((2, 2 * q, cols), F32),
            vm((2, 2 * q, cols), BF16),
            vm((q, cols), BF16),
            vm((q, cols), BF16),
            vm((q, cols), BF16),
            vm((q, cols), BF16),
            vm((q, cols), BF16),
            vm((q, cols), BF16),
            vm((2, rows, cols), BF16),
            vm((VISITS - 1, 8, lanes), F32),
            vm((VISITS - 1, 8, lanes), F32),
            vm((2, 8, lanes), F32),
            vm((2, 8, lanes), F32),
            pltpu.SemaphoreType.DMA((16,)),
            pltpu.SemaphoreType.DMA((3,)),
            pltpu.SemaphoreType.DMA((messages,)),
            pltpu.SemaphoreType.DMA((messages,)),
        ],
        compiler_params=pltpu.CompilerParams(
            collective_id=0, has_side_effects=True, vmem_limit_bytes=62 * 2**20
        ),
    )(xi, xt, wi, wt, scale, shift, partner)
    return pl.pallas_call(
        store,
        out_shape=(
            jax.ShapeDtypeStruct((rows, share), BF16),
            jax.ShapeDtypeStruct((rows, share), BF16),
            jax.ShapeDtypeStruct((rows,), F32),
        ),
        in_specs=[pl.BlockSpec(memory_space=pl.ANY)] * 3,
        out_specs=(pl.BlockSpec(memory_space=pl.ANY),) * 3,
        scratch_shapes=[vm((rows, share), BF16), vm((rows, share), BF16), vm((rows,), F32), pltpu.SemaphoreType.DMA((6,))],
        compiler_params=pltpu.CompilerParams(vmem_limit_bytes=62 * 2**20),
    )(gi, gt, loss)


def solution(mesh):
    placed = (P("dp", "mp"), P("dp", "mp"), P("mp", None), P("mp", None), P(), P(), P("dp", None))
    return jax.shard_map(
        functools.partial(shards, mesh.shape["dp"]),
        mesh=mesh,
        in_specs=placed,
        out_specs=(P("dp", "mp"), P("dp", "mp"), P("dp")),
        check_vma=False,
    )
```

time: 72.1 us -> 65 us (0.902)
  local copies, waits for them, and re-layouts: 6.92 us -> 0 us
    unnamed x13 -> x0, local copies, waits for them, and re-layouts: 6.92 us -> none
    pallas_call x1, Pallas kernels: 62.9 us -> 61.2 us  [shards(): pl.pallas_call(functools.partial(kernel, n), out_shape=(jax.ShapeDtypeStr...]
    pallas_call x0 -> x1, Pallas kernels: none -> 1.7 us  [shards(): pl.pallas_call(store, out_shape=(jax.ShapeDtypeStruct((rows, share), BF16...]
where the time goes in v2:
time: 65 us; the launch traced here: 64.8 us
  Pallas kernels  62.9 us (97%)
  between operations  1.93 us (3%)
    pallas_call x1, Pallas kernels, shards(): pl.pallas_call(functools.partial(kernel, n), out_shape=(jax.ShapeDtypeStr...  61.2 us
    pallas_call x1, Pallas kernels, shards(): pl.pallas_call(store, out_shape=(jax.ShapeDtypeStruct((rows, share), BF16...  1.7 us

profile of v2, /device:TPU:1, one launch (start us, length us, event | category | flops | bytes accessed | tf_op | source)
XLA Modules:
  0.0 64.8 jit_solution(12040127124680096784)
XLA Ops:
  1.9 61.2 %shard_map.94 = (bf16[192,384]{1,0:T(8,128)(2,1)}, bf16[192,384]{1,0:T(8,128)(2,1)}, f32[192]{0:T(256)}) custom-call(bf16[192,384]{1,0:T(8,128)(2,1)} %xi_hbm.1, bf16[192,384]{1,0:T(8,128)(2,1)} %xt_hbm.1, bf16[384,1536]{1,0:T(8,128)(2,1)} %wi_hbm.1, bf16[384,1536]{1,0:T(8,128)(2,1)} %wt_hbm.1, f32[1]{0:T(128)S(6)} %copy.10.scale_hbm, f32[1]{0:T(128)S(6)} %copy.11.shift_hbm, ...), custom_call_target="tpu_custom_call" | custom-call | tf_op jit(solution)/shard_map/pallas_call | solution.py:402
  63.1 1.7 %shard_map.95 = (bf16[192,384]{1,0:T(8,128)(2,1)}, bf16[192,384]{1,0:T(8,128)(2,1)}, f32[192]{0:T(256)}) custom-call(bf16[192,384]{1,0:T(8,128)(2,1)} %get-tuple-element.6.gi, bf16[192,384]{1,0:T(8,128)(2,1)} %get-tuple-element.7.gt, f32[192]{0:T(256)} %get-tuple-element.8.loss), custom_call_target="tpu_custom_call" | custom-call | tf_op jit(solution)/shard_map/pallas_call | solution.py:457

commit v3 on v2

--- a/solution.py
+++ b/solution.py
@@ -11,7 +11,7 @@
 STEPS = 8
 VISITS = STEPS // 2
 PARTS = 3
-WIDE = 512
+WIDE = 768
 
 norm_eps = 1e-06
 F32 = jnp.float32
@@ -52,6 +52,8 @@
     near = (c, mq)
     prev = ((c + n - 1) % n, mq)
     after = ((c + 1) % n, mq)
+    prev_same = ((c + n - 1) % n, m)
+    after_same = ((c + 1) % n, m)
     up = ((c + 2) % n, m)
     down = [((c + n - 2 * s) % n, m) for s in range(1, VISITS)]
 
@@ -67,7 +69,7 @@
         loads[name].start()
 
     barrier = pltpu.get_barrier_semaphore()
-    peers = [core, near, prev, after, up, down[0]]
+    peers = [core, near, prev, after, prev_same, after_same, up, down[0]]
     for peer in peers:
         pl.semaphore_signal(barrier, inc=1, device_id=peer, device_id_type=MESH)
 
@@ -255,17 +257,21 @@
         where = at(half * q + j * part, part)
         return dbown[block, where] + dbrecv[block, where].astype(F32)
 
-    beside1, beside0, over = [], [], []
+    skew, beside0, over = [], [], []
     swap[1].wait_recv()
     for j in pieces:
-        y1send[piece(j)] = chip_sum(1, lo, j).astype(BF16)
-        beside1.append(send(message(y1send.at[piece(j)], y1recv.at[piece(j)], near)))
+        here = piece(j)
+        y1send[here] = chip_sum(1, lo, j).astype(BF16)
+        skew.append(send(message(y1send.at[here], y1recv.at[here], after_same)))
+        xsend[here] = chip_sum(1, 1 - lo, j).astype(BF16)
+        over.append(send(message(xsend.at[here], xrecv.at[here], after)))
+    swap[0].wait_recv()
+    for j in pieces:
+        here = piece(j)
+        y0send[here] = chip_sum(0, 1 - lo, j).astype(BF16)
+        beside0.append(send(message(y0send.at[here], y0recv.at[here], near)))
     for span in spans(cols):
         da[:, span] = mm(slope[:last * q], b[:, span])
-    swap[0].wait_recv()
-    for j in pieces:
-        y0send[piece(j)] = chip_sum(0, 1 - lo, j).astype(BF16)
-        beside0.append(send(message(y0send.at[piece(j)], y0recv.at[piece(j)], near)))
 
     def add_way(s, j):
         ways[s + 1][j].wait_recv()
@@ -274,11 +280,6 @@
     def onward(s, j):
         rsend[s - 1, piece(j)] = add_way(s, j).astype(BF16)
         send(ways[s][j])
-
-    def cross(j):
-        beside1[j].wait_recv()
-        xsend[piece(j)] = (chip_sum(1, 1 - lo, j) + y1recv[piece(j)].astype(F32)).astype(BF16)
-        over.append(send(message(xsend.at[piece(j)], xrecv.at[piece(j)], after)))
 
     spread = (
         lax.broadcasted_iota(jnp.int32, (q, lsend.shape[2]), 1)
@@ -295,9 +296,37 @@
     for s in range(1, VISITS):
         lsend[s - 1] = as_lanes(losses[s])
         home.append(send(message(lsend.at[s - 1], lrecv.at[s - 1], down[s - 1])))
-    for j in pieces:
-        cross(j)
+    def tangent(t, step, j):
+        here = piece(j)
+        vec = unit[t, here]
+        radial = jnp.sum(vec * step, axis=1, keepdims=True)
+        return ((step - vec * radial) / radius[t, here, 0:1]).astype(BF16)
+
+    def gather(t, j, target, size=q, skip=0):
+        where = at(j * q + skip, size)
+        return message(delta.at[t, where], delta.at[t, where], target)
+
+    beyond = [[], []]
+    inside = [[], []]
+
+    def text_step(j):
+        here = piece(j)
+        skew[j].wait_recv()
+        over[j].wait_recv()
+        beside0[j].wait_recv()
+        step = chip_sum(0, lo, j) + y0recv[here].astype(F32)
+        step = step + (xrecv[here].astype(F32) + y1recv[here].astype(F32))
+        delta[1, at(m * q + j * part, part)] = tangent(1, step, j)
+        beyond[1].append(send(gather(1, m, near, part, j * part)))
+
+    def image_step(j):
+        delta[0, at(m * q + j * part, part)] = tangent(0, add_way(0, j), j)
+        beyond[0].append(send(gather(0, m, near, part, j * part)))
+
+    for j in pieces:
         onward(1, j)
+        text_step(j)
+    inside[1].append(send(gather(1, m, core)))
 
     total = as_lanes(losses[0])
     for s in range(1, VISITS):
@@ -306,35 +335,9 @@
     lstage[0] = total
     pair = send(message(lstage.at[0], lpeer.at[0], core))
 
-    def tangent(t, step, j):
-        here = piece(j)
-        vec = unit[t, here]
-        radial = jnp.sum(vec * step, axis=1, keepdims=True)
-        return ((step - vec * radial) / radius[t, here, 0:1]).astype(BF16)
-
-    def gather(t, j, target, size=q, skip=0):
-        where = at(j * q + skip, size)
-        return message(delta.at[t, where], delta.at[t, where], target)
-
-    beyond = [[], []]
-    inside = [[], []]
-
-    def text_step(j):
-        beside0[j].wait_recv()
-        over[j].wait_recv()
-        step = chip_sum(0, lo, j) + y0recv[piece(j)].astype(F32) + xrecv[piece(j)].astype(F32)
-        delta[1, at(m * q + j * part, part)] = tangent(1, step, j)
-        beyond[1].append(send(gather(1, m, near, part, j * part)))
-
-    def image_step(j):
-        delta[0, at(m * q + j * part, part)] = tangent(0, add_way(0, j), j)
-        beyond[0].append(send(gather(0, m, near, part, j * part)))
-
-    for j in pieces:
-        text_step(j)
+    for j in pieces:
         image_step(j)
-    for t in (1, 0):
-        inside[t].append(send(gather(t, m, core)))
+    inside[0].append(send(gather(0, m, core)))
 
     pair.wait_recv()
     lstage[1] = lstage[0] + lpeer[0]
@@ -349,12 +352,14 @@
 
     for t in (1, 0):
         inside[t][0].wait_recv()
+    for j in pieces:
+        beyond[1][j].wait_recv()
+        inside[1].append(send(gather(1, mq, core, part, j * part)))
     result(1, gt_ref, lo)
     result(0, gi_ref, lo)
     for j in pieces:
-        for t in (1, 0):
-            beyond[t][j].wait_recv()
-            inside[t].append(send(gather(t, mq, core, part, j * part)))
+        beyond[0][j].wait_recv()
+        inside[0].append(send(gather(0, mq, core, part, j * part)))
     pair.wait_recv()
     loss = (lstage[1] + lpeer[1]) * (1.0 / (STEPS * rows))
     loss_ref[...] = loss[0, 0:rows]

time: 65 us -> 62.7 us (0.965)
  Pallas kernels: 62.9 us -> 60.6 us
    pallas_call x1, Pallas kernels: 61.2 us -> 58.9 us  [shards(): pl.pallas_call(functools.partial(kernel, n), out_shape=(jax.ShapeDtypeStr...]
where the time goes in v3:
time: 62.7 us; the launch traced here: 62.5 us
  Pallas kernels  60.6 us (97%)
  between operations  1.93 us (3%)
    pallas_call x1, Pallas kernels, shards(): pl.pallas_call(functools.partial(kernel, n), out_shape=(jax.ShapeDtypeStr...  58.9 us
    pallas_call x1, Pallas kernels, shards(): pl.pallas_call(store, out_shape=(jax.ShapeDtypeStruct((rows, share), BF16...  1.7 us

profile of v3, /device:TPU:1, one launch (start us, length us, event | category | flops | bytes accessed | tf_op | source)
XLA Modules:
  0.0 62.5 jit_solution(9507341233069839921)
XLA Ops:
  1.9 58.9 %shard_map.94 = (bf16[192,384]{1,0:T(8,128)(2,1)}, bf16[192,384]{1,0:T(8,128)(2,1)}, f32[192]{0:T(256)}) custom-call(bf16[192,384]{1,0:T(8,128)(2,1)} %xi_hbm.1, bf16[192,384]{1,0:T(8,128)(2,1)} %xt_hbm.1, bf16[384,1536]{1,0:T(8,128)(2,1)} %wi_hbm.1, bf16[384,1536]{1,0:T(8,128)(2,1)} %wt_hbm.1, f32[1]{0:T(128)S(6)} %copy.10.scale_hbm, f32[1]{0:T(128)S(6)} %copy.11.shift_hbm, ...), custom_call_target="tpu_custom_call" | custom-call | tf_op jit(solution)/shard_map/pallas_call | solution.py:407
  60.8 1.7 %shard_map.95 = (bf16[192,384]{1,0:T(8,128)(2,1)}, bf16[192,384]{1,0:T(8,128)(2,1)}, f32[192]{0:T(256)}) custom-call(bf16[192,384]{1,0:T(8,128)(2,1)} %get-tuple-element.6.gi, bf16[192,384]{1,0:T(8,128)(2,1)} %get-tuple-element.7.gt, f32[192]{0:T(256)} %get-tuple-element.8.loss), custom_call_target="tpu_custom_call" | custom-call | tf_op jit(solution)/shard_map/pallas_call | solution.py:462

commit v4 on v3

v4 whole, which is shorter than its diff:
```python
import functools

import jax
import jax.numpy as jnp
from jax import lax
from jax.experimental import pallas as pl
from jax.experimental.pallas import tpu as pltpu
from jax.sharding import PartitionSpec as P

MESH = pl.DeviceIdType.MESH
STEPS = 8
VISITS = STEPS // 2
MESSAGES = 73
LEAVING = 24
PARTS = 3
CUTS = 1

norm_eps = 1e-06
F32 = jnp.float32
BF16 = jnp.bfloat16

NN = (((1,), (0,)), ((), ()))
NT = (((1,), (1,)), ((), ()))


def mm(a, b, dims=NN):
    return lax.dot_general(a, b, dims, preferred_element_type=F32)


def kernel(
    n,
    xi_hbm, xt_hbm, wi_hbm, wt_hbm, scale_hbm, shift_hbm, partner_hbm,
    gi_hbm, gt_hbm, loss_hbm,
    gi_ref, gt_ref, loss_ref, x, w, partner_ref, scale_ref, shift_ref, psend, pown, precv, ysend, yrecv, unit, radius,
    a, b, slope, slope_t, da, rsend, rrecv,
    dbsend, dbown, dbrecv, y1send, y1recv, y0send, y0recv, xsend, xrecv,
    delta, lsend, lrecv, lstage, lpeer,
    load_sem, out_sem, ss, rs,
):
    c = lax.axis_index("dp")
    m = lax.axis_index("mp")
    lo, k = m // 2, m % 2
    mq = (m + 2) % 4
    q = a.shape[1] // VISITS
    rows = 4 * q
    wide = w.shape[3]
    part = q // PARTS

    core = (c, m + 1 - 2 * k)
    near = (c, mq)
    prev = ((c + n - 1) % n, mq)
    after = ((c + 1) % n, mq)
    prev_same = ((c + n - 1) % n, m)
    after_same = ((c + 1) % n, m)
    up = ((c + 2) % n, m)
    down = [((c + n - 2 * s) % n, m) for s in range(1, VISITS)]

    loads = {}
    for i, (name, src, dst) in enumerate(
        [("x0", xi_hbm, x.at[0])]
        + [(f"w0{h}", wi_hbm.at[:, pl.ds(h * wide, wide)], w.at[0, h]) for h in range(CUTS)]
        + [("x1", xt_hbm, x.at[1])]
        + [(f"w1{h}", wt_hbm.at[:, pl.ds(h * wide, wide)], w.at[1, h]) for h in range(CUTS)]
        + [("p", partner_hbm, partner_ref), ("t", scale_hbm, scale_ref), ("b", shift_hbm, shift_ref)]
    ):
        loads[name] = pltpu.make_async_copy(src, dst, load_sem.at[i])
        loads[name].start()

    barrier = pltpu.get_barrier_semaphore()
    peers = [core, near, prev, after, prev_same, after_same, up, down[0]]
    for peer in peers:
        pl.semaphore_signal(barrier, inc=1, device_id=peer, device_id_type=MESH)

    slots = {}
    leaving = {}

    def message(src, dst, target):
        i = len(slots)
        copy = pltpu.make_async_remote_copy(
            src_ref=src, dst_ref=dst, send_sem=ss.at[i % LEAVING], recv_sem=rs.at[i],
            device_id=target, device_id_type=MESH,
        )
        slots[i] = copy
        return copy

    def send(copy):
        slot = next(i for i, other in slots.items() if other is copy) % LEAVING
        if slot in leaving:
            leaving.pop(slot).wait_send()
        copy.start()
        leaving[slot] = copy
        return copy

    def drain():
        while leaving:
            leaving.pop(next(iter(leaving))).wait_send()

    def at(start, size):
        return pl.ds(pl.multiple_of(start, 16), size)

    def piece(j, base=0):
        return pl.ds(base + j * part, part)

    pieces = range(PARTS)
    halves = range(CUTS)
    both = [(j, h) for j in pieces for h in halves]

    def project(t, chip, which, out, to, ready=False):
        left = x[t, at((2 * chip + which) * q, q), :]
        for h in halves:
            if not ready:
                loads[f"w{t}{h}"].wait()
            out[h] = mm(left, w[t, h]).astype(to)

    first = [[None, None], [None, None]]
    for t in range(2):
        loads[f"x{t}"].wait()
        project(t, 1 - lo, 1 - k, psend.at[t, 0], BF16)
        if t == 0:
            pl.semaphore_wait(barrier, len(peers))
        first[t][0] = send(message(psend.at[t, 0], precv.at[t, 0], core))
    for t in range(2):
        project(t, 1 - lo, k, pown.at[t, 0], F32, True)
    project(0, lo, 1 - k, psend.at[0, 1], BF16, True)
    first[0][1] = send(message(psend.at[0, 1], precv.at[0, 1], core))

    second = [[], []]

    def over_y(t):
        first[t][0].wait_recv()
        for j in pieces:
            here = piece(j)
            second[t].append([])
            for h in halves:
                own = pown[t, 0, h, here] + precv[t, 0, h, here].astype(F32)
                ysend[t, h, here] = own.astype(BF16)
                copy = message(ysend.at[t, h, here], yrecv.at[t, h, here], near)
                second[t][j].append(send(copy))

    over_y(0)
    over_y(1)
    project(1, lo, 1 - k, psend.at[1, 1], BF16, True)
    first[1][1] = send(message(psend.at[1, 1], precv.at[1, 1], core))
    for t in range(2):
        project(t, lo, k, pown.at[t, 1], F32, True)

    def normalise(t, j, out, to):
        here = piece(j)
        for copy in second[t][j]:
            copy.wait_recv()
        raw = [
            pown[t, 1, h, here] + precv[t, 1, h, here].astype(F32) + yrecv[t, h, here].astype(F32)
            for h in halves
        ]
        squares = sum(jnp.sum(r * r, axis=1, keepdims=True) for r in raw)
        size = jnp.sqrt(squares + norm_eps)
        radius[t, here] = jnp.broadcast_to(size, (part, radius.shape[2]))
        for h in halves:
            value = raw[h] / size
            unit[t, h, here] = value
            out[h, at(to, part)] = value.astype(BF16)

    def visit(s, j):
        return [
            message(a.at[h, piece(j, s * q)], a.at[h, piece(j, (s + 1) * q)], up) for h in halves
        ]

    def text(into, j, target, size, skip, block, h):
        return message(
            b.at[h, at(block * rows + j * q + skip, size)],
            b.at[h, at(into * rows + j * q + skip, size)],
            target,
        )

    def text_core(block, j):
        return [send(text(block, j, core, q, 0, block, h)) for h in halves]

    def go_on(s, j):
        for done, copy in zip(hops[s - 1][j], hops[s][j]):
            done.wait_recv()
            send(copy)

    hops = [[visit(s, j) for j in pieces] for s in range(VISITS - 1)]
    first[0][1].wait_recv()
    for j in pieces:
        normalise(0, j, a, j * part)
        for hop in hops[0][j]:
            send(hop)

    first[1][1].wait_recv()
    across, beside, relay, in_chip = [], [], [], []
    for j in pieces:
        normalise(1, j, b, m * q + j * part)
        across.append([send(text(1, m, prev, part, j * part, 0, h)) for h in halves])
        beside.append([send(text(0, m, near, part, j * part, 0, h)) for h in halves])
        go_on(1, j)
    in_chip += text_core(0, m)
    for j in pieces:
        for h, copy in zip(halves, across[j]):
            copy.wait_recv()
            relay.append(send(text(1, mq, near, part, j * part, 1, h)))
        go_on(2, j)
    in_chip += text_core(1, mq)
    for copy in sum(beside, []):
        copy.wait_recv()
    in_chip += text_core(0, mq)

    for name in "ptb":
        loads[name].wait()
    temperature = jnp.exp(jnp.full((q, 2 * rows), scale_ref[0], F32))
    shift = shift_ref[0]
    named = (
        lax.broadcasted_iota(jnp.int32, (2 * rows, rows), 0) == partner_ref[...]
    ).astype(BF16)
    own = (
        lax.broadcasted_iota(jnp.int32, (q, rows), 1)
        == lax.broadcasted_iota(jnp.int32, (q, rows), 0) + m * q
    )
    positive = mm(own.astype(BF16), named, NT) > 0.5
    drain()

    for (j, h), copy in zip(both, relay):
        copy.wait_recv()
        in_chip.append(send(text(1, m, core, part, j * part, 1, h)))
    for copy in sum(hops[2], []):
        copy.wait_recv()
    for copy in in_chip:
        copy.wait_recv()

    losses = {}
    last = VISITS - 1

    def score(s, scores):
        logits = temperature * scores + shift
        z = jnp.where(positive, -logits, logits) if s == 0 else logits
        u = jnp.exp(-jnp.abs(z))
        soft = jnp.maximum(z, 0.0) + jnp.log1p(u)
        sig = jnp.where(z >= 0.0, 1.0, u) / (1.0 + u)
        grade = temperature * sig
        if s == 0:
            grade = jnp.where(positive, -grade, grade)
        slope[s * q:(s + 1) * q] = grade.astype(BF16)
        slope_t[:, s * q:(s + 1) * q] = grade.T.astype(BF16)
        losses[s] = jnp.sum(soft, axis=1, keepdims=True)

    scores = sum(mm(a[h], b[h], NT) for h in halves)
    score(last, scores[last * q:])

    far = slope[last * q:]
    for h in halves:
        rsend[last - 1, h] = mm(far, b[h]).astype(BF16)

    def homeward(s, j, h):
        return message(rsend.at[s - 1, h, piece(j)], rrecv.at[s - 1, h, piece(j)], down[0])

    ways = {s: [[homeward(s, j, h) for h in halves] for j in pieces] for s in range(1, VISITS)}
    for way in sum(ways[last], []):
        send(way)
    for s in range(last):
        score(s, scores[s * q:(s + 1) * q])

    def text_side(block, which):
        return jnp.concatenate(
            [slope_t[at((2 * block + half) * 2 * q + which * q, q)] for half in range(2)], axis=0
        )

    swap = {}
    for block in (1, 0):
        left = text_side(block, 1 - k)
        for h in halves:
            dbsend[block, h] = mm(left, a[h]).astype(BF16)
        swap[block] = send(message(dbsend.at[block], dbrecv.at[block], core))
    for block in (1, 0):
        left = text_side(block, k)
        for h in halves:
            dbown[block, h] = mm(left, a[h])

    def chip_sum(block, half, j, h):
        where = at(half * q + j * part, part)
        return dbown[block, h, where] + dbrecv[block, h, where].astype(F32)

    skew, beside0, over = [], [], []

    def parcel(block, half, j, held, into, target):
        copies = []
        for h in halves:
            held[h, piece(j)] = chip_sum(block, half, j, h).astype(BF16)
            copies.append(send(message(held.at[h, piece(j)], into.at[h, piece(j)], target)))
        return copies

    swap[1].wait_recv()
    for j in pieces:
        skew.append(parcel(1, lo, j, y1send, y1recv, after_same))
        over.append(parcel(1, 1 - lo, j, xsend, xrecv, after))
    swap[0].wait_recv()
    for j in pieces:
        beside0.append(parcel(0, 1 - lo, j, y0send, y0recv, near))
    for h in halves:
        da[h] = mm(slope[:last * q], b[h])

    def add_way(s, j, h):
        return da[h, piece(j, s * q)] + rrecv[s, h, piece(j)].astype(F32)

    def onward(s, j):
        for h, came, copy in zip(halves, ways[s + 1][j], ways[s][j]):
            came.wait_recv()
            rsend[s - 1, h, piece(j)] = add_way(s, j, h).astype(BF16)
            send(copy)

    spread = (
        lax.broadcasted_iota(jnp.int32, (q, lsend.shape[2]), 1)
        == lax.broadcasted_iota(jnp.int32, (q, lsend.shape[2]), 0) + m * q
    )

    def as_lanes(column):
        line = jnp.sum(jnp.where(spread, column, 0.0), axis=0, keepdims=True)
        return jnp.broadcast_to(line, lsend.shape[1:])

    for j in pieces:
        onward(2, j)
    home = []
    for s in range(1, VISITS):
        lsend[s - 1] = as_lanes(losses[s])
        home.append(send(message(lsend.at[s - 1], lrecv.at[s - 1], down[s - 1])))
    def tangent(t, step, j):
        here = piece(j)
        vec = [unit[t, h, here] for h in halves]
        radial = sum(jnp.sum(vec[h] * step[h], axis=1, keepdims=True) for h in halves)
        size = radius[t, here, 0:1]
        for h in halves:
            moved = (step[h] - vec[h] * radial) / size
            delta[t, h, at(m * q + j * part, part)] = moved.astype(BF16)
            beyond[t].append(send(gather(t, m, near, part, j * part, h)))

    def gather(t, j, target, size, skip, h):
        where = at(j * q + skip, size)
        return message(delta.at[t, h, where], delta.at[t, h, where], target)

    def gather_core(t):
        return [send(gather(t, m, core, q, 0, h)) for h in halves]

    beyond = [[], []]
    inside = [[], []]

    def text_step(j):
        here = piece(j)
        for copy in skew[j] + over[j] + beside0[j]:
            copy.wait_recv()
        tangent(1, [
            chip_sum(0, lo, j, h) + y0recv[h, here].astype(F32)
            + (xrecv[h, here].astype(F32) + y1recv[h, here].astype(F32))
            for h in halves
        ], j)

    def image_step(j):
        for copy in ways[1][j]:
            copy.wait_recv()
        tangent(0, [add_way(0, j, h) for h in halves], j)

    for j in pieces:
        onward(1, j)
        text_step(j)
    inside[1] += gather_core(1)

    total = as_lanes(losses[0])
    for s in range(1, VISITS):
        home[s - 1].wait_recv()
        total = total + lrecv[s - 1]
    lstage[0] = total
    pair = send(message(lstage.at[0], lpeer.at[0], core))

    for j in pieces:
        image_step(j)
    inside[0] += gather_core(0)

    pair.wait_recv()
    lstage[1] = lstage[0] + lpeer[0]
    pair = send(message(lstage.at[1], lpeer.at[1], near))
    drain()

    def result(t, out, chip):
        where = at(chip * 2 * q, 2 * q)
        out[where] = sum(mm(delta[t, h, where], w[t, h], NT) for h in halves).astype(BF16)

    for t in (1, 0):
        for copy in inside[t]:
            copy.wait_recv()
    for (j, h), copy in zip(both, beyond[1]):
        copy.wait_recv()
        inside[1].append(send(gather(1, mq, core, part, j * part, h)))
    result(1, gt_ref, lo)
    result(0, gi_ref, lo)
    for (j, h), copy in zip(both, beyond[0]):
        copy.wait_recv()
        inside[0].append(send(gather(0, mq, core, part, j * part, h)))
    pair.wait_recv()
    loss = (lstage[1] + lpeer[1]) * (1.0 / (STEPS * rows))
    loss_ref[...] = loss[0, 0:rows]
    stores = []

    def put(src, dst):
        copy = pltpu.make_async_copy(src, dst, out_sem.at[len(stores)])
        copy.start()
        stores.append(copy)

    put(loss_ref, loss_hbm)
    for t, out, out_hbm in ((1, gt_ref, gt_hbm), (0, gi_ref, gi_hbm)):
        for copy in inside[t][CUTS:]:
            copy.wait_recv()
        result(t, out, 1 - lo)
        put(out, out_hbm)
    drain()
    for copy in stores:
        copy.wait()


def store(gi, gt, loss, gi_out, gt_out, loss_out, gi_held, gt_held, loss_held, sem):
    held = (gi_held, gt_held, loss_held)
    ins = [pltpu.make_async_copy(s, d, sem.at[i]) for i, (s, d) in enumerate(zip((gi, gt, loss), held))]
    outs = [
        pltpu.make_async_copy(s, d, sem.at[3 + i])
        for i, (s, d) in enumerate(zip(held, (gi_out, gt_out, loss_out)))
    ]
    for copy in ins:
        copy.start()
    for into, out in zip(ins, outs):
        into.wait()
        out.start()
    for out in outs:
        out.wait()


def shards(n, xi, xt, wi, wt, scale, shift, partner):
    rows, share = xi.shape
    wide = wi.shape[1] // CUTS
    q = rows // 4
    vm = pltpu.VMEM
    lanes = -(-rows // 128) * 128
    gi, gt, loss = pl.pallas_call(
        functools.partial(kernel, n),
        out_shape=(
            jax.ShapeDtypeStruct((rows, share), BF16),
            jax.ShapeDtypeStruct((rows, share), BF16),
            jax.ShapeDtypeStruct((rows,), F32),
        ),
        in_specs=[pl.BlockSpec(memory_space=pl.ANY)] * 7,
        out_specs=(pl.BlockSpec(memory_space=pl.ANY),) * 3,
        scratch_shapes=[
            vm((rows, share), BF16),
            vm((rows, share), BF16),
            vm((rows,), F32),
            vm((2, rows, share), BF16),
            vm((2, CUTS, share, wide), BF16),
            vm((1, rows), jnp.int32),
            pltpu.SMEM((1,), F32),
            pltpu.SMEM((1,), F32),
            vm((2, 2, CUTS, q, wide), BF16),
            vm((2, 2, CUTS, q, wide), F32),
            vm((2, 2, CUTS, q, wide), BF16),
            vm((2, CUTS, q, wide), BF16),
            vm((2, CUTS, q, wide), BF16),
            vm((2, CUTS, q, wide), F32),
            vm((2, q, 128), F32),
            vm((CUTS, VISITS * q, wide), BF16),
            vm((CUTS, 2 * rows, wide), BF16),
            vm((VISITS * q, 2 * rows), BF16),
            vm((2 * rows, VISITS * q), BF16),
            vm((CUTS, (VISITS - 1) * q, wide), F32),
            vm((VISITS - 1, CUTS, q, wide), BF16),
            vm((VISITS - 1, CUTS, q, wide), BF16),
            vm((2, CUTS, 2 * q, wide), BF16),
            vm((2, CUTS, 2 * q, wide), F32),
            vm((2, CUTS, 2 * q, wide), BF16),
            vm((CUTS, q, wide), BF16),
            vm((CUTS, q, wide), BF16),
            vm((CUTS, q, wide), BF16),
            vm((CUTS, q, wide), BF16),
            vm((CUTS, q, wide), BF16),
            vm((CUTS, q, wide), BF16),
            vm((2, CUTS, rows, wide), BF16),
            vm((VISITS - 1, 8, lanes), F32),
            vm((VISITS - 1, 8, lanes), F32),
            vm((2, 8, lanes), F32),
            vm((2, 8, lanes), F32),
            pltpu.SemaphoreType.DMA((5 + 2 * CUTS,)),
            pltpu.SemaphoreType.DMA((3,)),
            pltpu.SemaphoreType.DMA((LEAVING,)),
            pltpu.SemaphoreType.DMA((MESSAGES,)),
        ],
        compiler_params=pltpu.CompilerParams(
            collective_id=0, has_side_effects=True, vmem_limit_bytes=62 * 2**20
        ),
    )(xi, xt, wi, wt, scale, shift, partner)
    return pl.pallas_call(
        store,
        out_shape=(
            jax.ShapeDtypeStruct((rows, share), BF16),
            jax.ShapeDtypeStruct((rows, share), BF16),
            jax.ShapeDtypeStruct((rows,), F32),
        ),
        in_specs=[pl.BlockSpec(memory_space=pl.ANY)] * 3,
        out_specs=(pl.BlockSpec(memory_space=pl.ANY),) * 3,
        scratch_shapes=[vm((rows, share), BF16), vm((rows, share), BF16), vm((rows,), F32), pltpu.SemaphoreType.DMA((6,))],
        compiler_params=pltpu.CompilerParams(vmem_limit_bytes=62 * 2**20),
    )(gi, gt, loss)


def solution(mesh):
    placed = (P("dp", "mp"), P("dp", "mp"), P("mp", None), P("mp", None), P(), P(), P("dp", None))
    return jax.shard_map(
        functools.partial(shards, mesh.shape["dp"]),
        mesh=mesh,
        in_specs=placed,
        out_specs=(P("dp", "mp"), P("dp", "mp"), P("dp")),
        check_vma=False,
    )
```

time: 62.7 us -> 61.3 us (0.978)
  Pallas kernels: 60.6 us -> 59.2 us
    pallas_call x1, Pallas kernels: 58.9 us -> 57.5 us  [shards(): pl.pallas_call(functools.partial(kernel, n), out_shape=(jax.ShapeDtypeStr...]
where the time goes in v4:
time: 61.3 us; the launch traced here: 61.1 us
  Pallas kernels  59.2 us (97%)
  between operations  1.93 us (3%)
    pallas_call x1, Pallas kernels, shards(): pl.pallas_call(functools.partial(kernel, n), out_shape=(jax.ShapeDtypeStr...  57.5 us
    pallas_call x1, Pallas kernels, shards(): pl.pallas_call(store, out_shape=(jax.ShapeDtypeStruct((rows, share), BF16...  1.7 us

profile of v4, /device:TPU:1, one launch (start us, length us, event | category | flops | bytes accessed | tf_op | source)
XLA Modules:
  0.0 61.1 jit_solution(9668304620337858832)
XLA Ops:
  1.9 57.5 %shard_map.94 = (bf16[192,384]{1,0:T(8,128)(2,1)}, bf16[192,384]{1,0:T(8,128)(2,1)}, f32[192]{0:T(256)}) custom-call(bf16[192,384]{1,0:T(8,128)(2,1)} %xi_hbm.1, bf16[192,384]{1,0:T(8,128)(2,1)} %xt_hbm.1, bf16[384,1536]{1,0:T(8,128)(2,1)} %wi_hbm.1, bf16[384,1536]{1,0:T(8,128)(2,1)} %wt_hbm.1, f32[1]{0:T(128)S(6)} %copy.10.scale_hbm, f32[1]{0:T(128)S(6)} %copy.11.shift_hbm, ...), custom_call_target="tpu_custom_call" | custom-call | tf_op jit(solution)/shard_map/pallas_call | solution.py:439
  59.4 1.7 %shard_map.95 = (bf16[192,384]{1,0:T(8,128)(2,1)}, bf16[192,384]{1,0:T(8,128)(2,1)}, f32[192]{0:T(256)}) custom-call(bf16[192,384]{1,0:T(8,128)(2,1)} %get-tuple-element.6.gi, bf16[192,384]{1,0:T(8,128)(2,1)} %get-tuple-element.7.gt, f32[192]{0:T(256)} %get-tuple-element.8.loss), custom_call_target="tpu_custom_call" | custom-call | tf_op jit(solution)/shard_map/pallas_call | solution.py:494

commit v5 on v4

--- a/solution.py
+++ b/solution.py
@@ -10,7 +10,7 @@
 MESH = pl.DeviceIdType.MESH
 STEPS = 8
 VISITS = STEPS // 2
-MESSAGES = 73
+TICKETS = 54
 LEAVING = 24
 PARTS = 3
 CUTS = 1
@@ -73,11 +73,17 @@
 
     slots = {}
     leaving = {}
-
-    def message(src, dst, target):
+    taken = [0]
+
+    def ticket():
+        taken[0] += 1
+        return taken[0] - 1
+
+    def message(src, dst, target, shared=None):
         i = len(slots)
         copy = pltpu.make_async_remote_copy(
-            src_ref=src, dst_ref=dst, send_sem=ss.at[i % LEAVING], recv_sem=rs.at[i],
+            src_ref=src, dst_ref=dst, send_sem=ss.at[i % LEAVING],
+            recv_sem=rs.at[ticket() if shared is None else shared],
             device_id=target, device_id_type=MESH,
         )
         slots[i] = copy
@@ -94,6 +100,12 @@
     def drain():
         while leaving:
             leaving.pop(next(iter(leaving))).wait_send()
+
+    def arrival(ref, shared):
+        pltpu.make_async_remote_copy(
+            src_ref=ref, dst_ref=ref, send_sem=ss.at[0], recv_sem=rs.at[shared],
+            device_id=core, device_id_type=MESH,
+        ).wait_recv()
 
     def at(start, size):
         return pl.ds(pl.multiple_of(start, 16), size)
@@ -160,20 +172,27 @@
             unit[t, h, here] = value
             out[h, at(to, part)] = value.astype(BF16)
 
+    final = ticket()
+
     def visit(s, j):
+        shared = final if s == VISITS - 2 else None
         return [
-            message(a.at[h, piece(j, s * q)], a.at[h, piece(j, (s + 1) * q)], up) for h in halves
+            message(a.at[h, piece(j, s * q)], a.at[h, piece(j, (s + 1) * q)], up, shared)
+            for h in halves
         ]
 
-    def text(into, j, target, size, skip, block, h):
+    in_chip, beside = ticket(), ticket()
+
+    def text(into, j, target, size, skip, block, h, shared=None):
         return message(
             b.at[h, at(block * rows + j * q + skip, size)],
             b.at[h, at(into * rows + j * q + skip, size)],
-            target,
+            target, shared,
         )
 
     def text_core(block, j):
-        return [send(text(block, j, core, q, 0, block, h)) for h in halves]
+        for h in halves:
+            send(text(block, j, core, q, 0, block, h, in_chip))
 
     def go_on(s, j):
         for done, copy in zip(hops[s - 1][j], hops[s][j]):
@@ -188,22 +207,22 @@
             send(hop)
 
     first[1][1].wait_recv()
-    across, beside, relay, in_chip = [], [], [], []
+    across, relay = [], []
     for j in pieces:
         normalise(1, j, b, m * q + j * part)
         across.append([send(text(1, m, prev, part, j * part, 0, h)) for h in halves])
-        beside.append([send(text(0, m, near, part, j * part, 0, h)) for h in halves])
+        for h in halves:
+            send(text(0, m, near, part, j * part, 0, h, beside))
         go_on(1, j)
-    in_chip += text_core(0, m)
+    text_core(0, m)
     for j in pieces:
         for h, copy in zip(halves, across[j]):
             copy.wait_recv()
             relay.append(send(text(1, mq, near, part, j * part, 1, h)))
         go_on(2, j)
-    in_chip += text_core(1, mq)
-    for copy in sum(beside, []):
-        copy.wait_recv()
-    in_chip += text_core(0, mq)
+    text_core(1, mq)
+    arrival(b.at[:, at(mq * q, q)], beside)
+    text_core(0, mq)
 
     for name in "ptb":
         loads[name].wait()
@@ -221,11 +240,9 @@
 
     for (j, h), copy in zip(both, relay):
         copy.wait_recv()
-        in_chip.append(send(text(1, m, core, part, j * part, 1, h)))
-    for copy in sum(hops[2], []):
-        copy.wait_recv()
-    for copy in in_chip:
-        copy.wait_recv()
+        send(text(1, m, core, part, j * part, 1, h, in_chip))
+    arrival(a.at[:, pl.ds((VISITS - 1) * q, q)], final)
+    arrival(b.at[:, pl.ds(0, 4 * q)], in_chip)
 
     losses = {}
     last = VISITS - 1
@@ -279,22 +296,20 @@
         where = at(half * q + j * part, part)
         return dbown[block, h, where] + dbrecv[block, h, where].astype(F32)
 
-    skew, beside0, over = [], [], []
+    shares = [ticket() for _ in pieces]
 
     def parcel(block, half, j, held, into, target):
-        copies = []
         for h in halves:
             held[h, piece(j)] = chip_sum(block, half, j, h).astype(BF16)
-            copies.append(send(message(held.at[h, piece(j)], into.at[h, piece(j)], target)))
-        return copies
+            send(message(held.at[h, piece(j)], into.at[h, piece(j)], target, shares[j]))
 
     swap[1].wait_recv()
     for j in pieces:
-        skew.append(parcel(1, lo, j, y1send, y1recv, after_same))
-        over.append(parcel(1, 1 - lo, j, xsend, xrecv, after))
+        parcel(1, lo, j, y1send, y1recv, after_same)
+        parcel(1, 1 - lo, j, xsend, xrecv, after)
     swap[0].wait_recv()
     for j in pieces:
-        beside0.append(parcel(0, 1 - lo, j, y0send, y0recv, near))
+        parcel(0, 1 - lo, j, y0send, y0recv, near)
     for h in halves:
         da[h] = mm(slope[:last * q], b[h])
 
@@ -332,9 +347,11 @@
             delta[t, h, at(m * q + j * part, part)] = moved.astype(BF16)
             beyond[t].append(send(gather(t, m, near, part, j * part, h)))
 
-    def gather(t, j, target, size, skip, h):
+    handed = [ticket(), ticket()]
+
+    def gather(t, j, target, size, skip, h, shared=None):
         where = at(j * q + skip, size)
-        return message(delta.at[t, h, where], delta.at[t, h, where], target)
+        return message(delta.at[t, h, where], delta.at[t, h, where], target, shared)
 
     def gather_core(t):
         return [send(gather(t, m, core, q, 0, h)) for h in halves]
@@ -344,8 +361,7 @@
 
     def text_step(j):
         here = piece(j)
-        for copy in skew[j] + over[j] + beside0[j]:
-            copy.wait_recv()
+        arrival(y1recv.at[:, pl.ds(0, 3 * part)], shares[j])
         tangent(1, [
             chip_sum(0, lo, j, h) + y0recv[h, here].astype(F32)
             + (xrecv[h, here].astype(F32) + y1recv[h, here].astype(F32))
@@ -387,12 +403,12 @@
             copy.wait_recv()
     for (j, h), copy in zip(both, beyond[1]):
         copy.wait_recv()
-        inside[1].append(send(gather(1, mq, core, part, j * part, h)))
+        send(gather(1, mq, core, part, j * part, h, handed[1]))
     result(1, gt_ref, lo)
     result(0, gi_ref, lo)
     for (j, h), copy in zip(both, beyond[0]):
         copy.wait_recv()
-        inside[0].append(send(gather(0, mq, core, part, j * part, h)))
+        send(gather(0, mq, core, part, j * part, h, handed[0]))
     pair.wait_recv()
     loss = (lstage[1] + lpeer[1]) * (1.0 / (STEPS * rows))
     loss_ref[...] = loss[0, 0:rows]
@@ -405,8 +421,7 @@
 
     put(loss_ref, loss_hbm)
     for t, out, out_hbm in ((1, gt_ref, gt_hbm), (0, gi_ref, gi_hbm)):
-        for copy in inside[t][CUTS:]:
-            copy.wait_recv()
+        arrival(delta.at[t, :, at((m + 3 - 2 * k) % 4 * q, q)], handed[t])
         result(t, out, 1 - lo)
         put(out, out_hbm)
     drain()
@@ -485,7 +500,7 @@
             pltpu.SemaphoreType.DMA((5 + 2 * CUTS,)),
             pltpu.SemaphoreType.DMA((3,)),
             pltpu.SemaphoreType.DMA((LEAVING,)),
-            pltpu.SemaphoreType.DMA((MESSAGES,)),
+            pltpu.SemaphoreType.DMA((TICKETS,)),
         ],
         compiler_params=pltpu.CompilerParams(
             collective_id=0, has_side_effects=True, vmem_limit_bytes=62 * 2**20

time: 61.3 us -> 61.1 us (level)
  no operation moved by 1% of the time
where the time goes in v5:
time: 61.1 us; the launch traced here: 60.9 us
  Pallas kernels  59 us (97%)
  between operations  1.93 us (3%)
    pallas_call x1, Pallas kernels, shards(): pl.pallas_call(functools.partial(kernel, n), out_shape=(jax.ShapeDtypeStr...  57.3 us
    pallas_call x1, Pallas kernels, shards(): pl.pallas_call(store, out_shape=(jax.ShapeDtypeStruct((rows, share), BF16...  1.7 us

profile of v5, /device:TPU:1, one launch (start us, length us, event | category | flops | bytes accessed | tf_op | source)
XLA Modules:
  0.0 60.9 jit_solution(17530390965975756289)
XLA Ops:
  1.9 57.3 %shard_map.94 = (bf16[192,384]{1,0:T(8,128)(2,1)}, bf16[192,384]{1,0:T(8,128)(2,1)}, f32[192]{0:T(256)}) custom-call(bf16[192,384]{1,0:T(8,128)(2,1)} %xi_hbm.1, bf16[192,384]{1,0:T(8,128)(2,1)} %xt_hbm.1, bf16[384,1536]{1,0:T(8,128)(2,1)} %wi_hbm.1, bf16[384,1536]{1,0:T(8,128)(2,1)} %wt_hbm.1, f32[1]{0:T(128)S(6)} %copy.10.scale_hbm, f32[1]{0:T(128)S(6)} %copy.11.shift_hbm, ...), custom_call_target="tpu_custom_call" | custom-call | tf_op jit(solution)/shard_map/pallas_call | solution.py:454
  59.2 1.7 %shard_map.95 = (bf16[192,384]{1,0:T(8,128)(2,1)}, bf16[192,384]{1,0:T(8,128)(2,1)}, f32[192]{0:T(256)}) custom-call(bf16[192,384]{1,0:T(8,128)(2,1)} %get-tuple-element.6.gi, bf16[192,384]{1,0:T(8,128)(2,1)} %get-tuple-element.7.gt, f32[192]{0:T(256)} %get-tuple-element.8.loss), custom_call_target="tpu_custom_call" | custom-call | tf_op jit(solution)/shard_map/pallas_call | solution.py:509

commit v6 on v5

--- a/solution.py
+++ b/solution.py
@@ -50,7 +50,6 @@
     near = (c, mq)
     prev = ((c + n - 1) % n, mq)
     after = ((c + 1) % n, mq)
-    prev_same = ((c + n - 1) % n, m)
     after_same = ((c + 1) % n, m)
     up = ((c + 2) % n, m)
     down = [((c + n - 2 * s) % n, m) for s in range(1, VISITS)]
@@ -67,7 +66,7 @@
         loads[name].start()
 
     barrier = pltpu.get_barrier_semaphore()
-    peers = [core, near, prev, after, prev_same, after_same, up, down[0]]
+    peers = [core, near, after, down[0]]
     for peer in peers:
         pl.semaphore_signal(barrier, inc=1, device_id=peer, device_id_type=MESH)
 

time: 61.1 us -> 60.5 us (level)
    pallas_call x1, Pallas kernels: 57.3 us -> 56.7 us  [shards(): pl.pallas_call(functools.partial(kernel, n), out_shape=(jax.ShapeDtypeStr...]
where the time goes in v6:
time: 60.5 us; the launch traced here: 60.3 us
  Pallas kernels  58.4 us (97%)
  between operations  1.93 us (3%)
    pallas_call x1, Pallas kernels, shards(): pl.pallas_call(functools.partial(kernel, n), out_shape=(jax.ShapeDtypeStr...  56.7 us
    pallas_call x1, Pallas kernels, shards(): pl.pallas_call(store, out_shape=(jax.ShapeDtypeStruct((rows, share), BF16...  1.7 us

profile of v6, /device:TPU:1, one launch (start us, length us, event | category | flops | bytes accessed | tf_op | source)
XLA Modules:
  0.0 60.3 jit_solution(7926577643835889258)
XLA Ops:
  1.9 56.7 %shard_map.94 = (bf16[192,384]{1,0:T(8,128)(2,1)}, bf16[192,384]{1,0:T(8,128)(2,1)}, f32[192]{0:T(256)}) custom-call(bf16[192,384]{1,0:T(8,128)(2,1)} %xi_hbm.1, bf16[192,384]{1,0:T(8,128)(2,1)} %xt_hbm.1, bf16[384,1536]{1,0:T(8,128)(2,1)} %wi_hbm.1, bf16[384,1536]{1,0:T(8,128)(2,1)} %wt_hbm.1, f32[1]{0:T(128)S(6)} %copy.10.scale_hbm, f32[1]{0:T(128)S(6)} %copy.11.shift_hbm, ...), custom_call_target="tpu_custom_call" | custom-call | tf_op jit(solution)/shard_map/pallas_call | solution.py:453
  58.6 1.7 %shard_map.95 = (bf16[192,384]{1,0:T(8,128)(2,1)}, bf16[192,384]{1,0:T(8,128)(2,1)}, f32[192]{0:T(256)}) custom-call(bf16[192,384]{1,0:T(8,128)(2,1)} %get-tuple-element.6.gi, bf16[192,384]{1,0:T(8,128)(2,1)} %get-tuple-element.7.gt, f32[192]{0:T(256)} %get-tuple-element.8.loss), custom_call_target="tpu_custom_call" | custom-call | tf_op jit(solution)/shard_map/pallas_call | solution.py:508
